TPU v7x, 256 devices: a whole 4x4x8 slice. The times are simulated.
256 devices in a mesh: depth: 32 (over x, y, core), tile: 8 (over z).
Axes of the slice: x: 4, y: 4, z: 8, core: 2. Of those that a mesh axis runs over, the one named last changes fastest.
Arguments:
- pressure_old: float32 [256, 512, 1024], P('depth', 'tile'), may hold values from -6 to 6
- pressure_now: float32 [256, 512, 1024], P('depth', 'tile'), may hold values from -6 to 6
- solid_flags: int32 [256, 512, 1024], P('depth', 'tile'), may hold values 0 or 1
Outputs:
- pressure_mid: float32 [256, 512, 1024], P('depth', 'tile')
- pressure_new: float32 [256, 512, 1024], P('depth', 'tile')
- image: float32 [4, 512, 1024], P(None, 'tile')
All inputs are finite; a program needn't handle non-finite values. No bound on the sum of `solid_flags` on one device may be relied on, other than what follows from the above.
Results may differ from a plain program's by a relative error of at most 0.00005.
Values sent between devices are 32-bit elements; how exact they have to be, the bound alone decides.
A program may use at most 64 MiB of HBM per device.

v0:
```python
import jax
import jax.numpy as jnp
from jax import lax
from jax.sharding import PartitionSpec as P


def padded_2(cells, sides, width):
    for axis, dim in sides:
        count = lax.axis_size(axis)
        ends = count - 1
        head = lax.slice_in_dim(cells, 0, width, axis=dim)
        tail = lax.slice_in_dim(cells, cells.shape[dim] - width, cells.shape[dim], axis=dim)
        cells = jnp.concatenate(
            [
                lax.ppermute(tail, axis, [(i, (i + 1) % count) for i in range(ends)]),
                cells,
                lax.ppermute(head, axis, [((i + 1) % count, i) for i in range(ends)]),
            ],
            axis=dim,
        )
    return cells


def prefix(x, axis, combine, identity):
    size, here = (lax.axis_size(axis), lax.axis_index(axis))
    everything = lax.all_gather(x, axis)
    start = jnp.broadcast_to(jnp.asarray(identity, x.dtype), x.shape)

    def lap(k, before):
        reached = k < here
        new = combine(before, everything[k])
        return jnp.where(reached, new, before)

    return lax.fori_loop(0, size, lap, start)


def advance(previous, extended, open_field):
    padded = jnp.pad(extended, ((0, 0), (0, 0), (1, 1)))
    current = padded[1:-1, 1:-1, 1:-1]
    beside = padded[2:, 1:-1, 1:-1] + padded[:-2, 1:-1, 1:-1]
    beside = beside + padded[1:-1, 2:, 1:-1] + padded[1:-1, :-2, 1:-1]
    beside = beside + padded[1:-1, 1:-1, 2:] + padded[1:-1, 1:-1, :-2]
    return open_field * (2.0 * current - previous + 0.3 * (beside - 6.0 * current))


def faces(field):
    return padded_2(field, (("depth", 0), ("tile", 1)), 1)


def add_pair(earlier, later):
    return earlier + later


def shards(pressure_old, pressure_now, solid_flags):
    open_field = (1 - solid_flags).astype(jnp.float32)
    pressure_mid = advance(pressure_old, faces(pressure_now), open_field)
    pressure_new = advance(pressure_now, faces(pressure_mid), open_field)
    grid_depth = pressure_new.shape[0] * lax.axis_size("depth")
    square = pressure_new * pressure_new
    tau = 4.0 / grid_depth * square / (1.0 + square)
    weight = (1.0 - jnp.exp(-tau)) * jnp.exp(-(jnp.cumsum(tau, axis=0) - tau))
    red = jnp.sum(jax.nn.sigmoid(3.0 * pressure_new) * weight, axis=0)
    green = jnp.sum(jnp.exp(-0.5 * square) * weight, axis=0)
    blue = jnp.sum(jax.nn.sigmoid(-3.0 * pressure_new) * weight, axis=0)
    colours = jnp.stack([red, green, blue])
    own_depth = jnp.sum(tau, axis=0)
    prior = prefix(own_depth, "depth", add_pair, jnp.zeros_like(own_depth))
    attenuated = colours * jnp.exp(-prior)[None]
    shaded, total = lax.psum((attenuated, own_depth), "depth")
    image = jnp.concatenate([shaded, (1.0 - jnp.exp(-total))[None]], axis=0)
    return (pressure_mid, pressure_new, image)


def solution(mesh):
    return jax.shard_map(
        shards,
        mesh=mesh,
        in_specs=(P("depth", "tile", None), P("depth", "tile", None), P("depth", "tile", None)),
        out_specs=(P("depth", "tile", None), P("depth", "tile", None), P(None, "tile", None)),
        check_vma=False,
    )
```

profile of v0, /device:TPU:1, one launch (start us, length us, event | category | flops | bytes accessed | tf_op | source)
XLA Modules:
  0.0 285.5 jit_solution(4166600996416146702)
XLA Ops:
  7.2 1.1 fusion.20
  8.3 4.6 %collective-permute-start.1 = (f32[1,64,1024]{2,1,0:T(8,128)S(1)}, f32[1,64,1024]{2,1,0:T(8,128)S(1)}, u32[]{:S(2)}, u32[]{:S(2)}) collective-permute-start(f32[1,64,1024]{2,1,0:T(8,128)S(1)} %get-tuple-element.119), channel_id=1, source_target_pairs={{0,8},{8,16},{16,24},{24,32},{32,40},{40,48},{48,56},{56,64},{64,7... | collective-permute-start | bytes 786440 | tf_op jit(solution)/shard_map/ppermute | solution.py:15
  12.9 1.9 collective-permute-start
  14.8 1.4 collective-permute-done.1
  16.2 1.7 constant_dynamic-update-slice_fusion.1
  17.9 2.6 collective-permute-done
  20.7 1.4 collective-permute-start.2
  22.1 4.4 %collective-permute-start.3 = (f32[10,1,1024]{2,1,0:T(1,128)S(1)}, f32[10,1,1024]{2,1,0:T(1,128)S(1)}, u32[]{:S(2)}, u32[]{:S(2)}) collective-permute-start(f32[10,1,1024]{2,1,0:T(1,128)S(1)} %get-tuple-element.114), channel_id=1, source_target_pairs={{0,1},{1,2},{2,3},{3,4},{4,5},{5,6},{6,7},{8,9},{9,10},{10,11},{11... | collective-permute-start | bytes 122888 | tf_op jit(solution)/shard_map/ppermute | solution.py:15
  26.6 1.1 collective-permute-done.3
  27.6 1.3 select_maximum_fusion.4
  29.0 2.5 fusion.11
  31.5 1.9 collective-permute-start.4
  33.5 3.6 %collective-permute-start.5 = (f32[1,64,1024]{2,1,0:T(8,128)S(1)}, f32[1,64,1024]{2,1,0:T(8,128)S(1)}, u32[]{:S(2)}, u32[]{:S(2)}) collective-permute-start(f32[1,64,1024]{2,1,0:T(8,128)S(1)} %get-tuple-element.116), channel_id=1, source_target_pairs={{0,8},{8,16},{16,24},{24,32},{32,40},{40,48},{48,56},{56,64},{64,7... | collective-permute-start | bytes 786440 | tf_op jit(solution)/shard_map/ppermute | solution.py:15
  37.1 2.1 collective-permute-done.4
  39.2 1.2 collective-permute-done.5
  40.5 1.3 collective-permute-start.6
  41.8 4.3 %collective-permute-start.7 = (f32[10,1,1024]{2,1,0:T(1,128)S(1)}, f32[10,1,1024]{2,1,0:T(1,128)S(1)}, u32[]{:S(2)}, u32[]{:S(2)}) collective-permute-start(f32[10,1,1024]{2,1,0:T(1,128)S(1)} %get-tuple-element.112), channel_id=1, source_target_pairs={{0,1},{1,2},{2,3},{3,4},{4,5},{5,6},{6,7},{8,9},{9,10},{10,11},{11... | collective-permute-start | bytes 122888 | tf_op jit(solution)/shard_map/ppermute | solution.py:15
  46.1 1.1 collective-permute-done.7
  47.2 3.1 %select_maximum_fusion = f32[10,66,1026]{2,1,0:T(8,128)S(1)} fusion(f32[10,1,1024]{2,1,0:T(1,128)S(1)} %collective-permute-done.6, f32[10,1,1024]{2,1,0:T(1,128)S(1)} %collective-permute-done.7, f32[1,64,1024]{2,1,0:T(8,128)S(1)} %collective-permute-done.4, f32[8,64,1024]{2,1,0:T(8,128)S(1)} %fusion.11, f32[1,64,1024]{2,1,0:T(8,128)S(1)} %collective-permute-done.5), kind=kLoop, calls=%fused_computation.3 | loop fusion | flops 8125920 | bytes 5412000 | tf_op jit(solution)/shard_map/concatenate | solution.py:13
  50.2 2.3 fusion.4
  52.6 3.7 %multiply_reduce_fusion.2 = (f32[64,1024]{1,0:T(8,128)S(1)}, f32[64,1024]{1,0:T(8,128)S(1)}, f32[64,1024]{1,0:T(8,128)S(1)}, f32[64,1024]{1,0:T(8,128)}) fusion(f32[8,64,1024]{2,1,0:T(8,128)S(1)} %fusion.4), kind=kOutput, calls=%fused_computation.42 | output fusion | flops 18612224 | bytes 3145728 | tf_op jit(solution)/shard_map/jit(cumsum)/reduce_window_sum | solution.py:61
  56.4 69.4 %all-gather.3.cloned.1.call-done = f32[2048,1024]{1,0:T(8,128)} async-done(((f32[64,1024]{1,0:T(8,128)}), f32[2048,1024]{1,0:T(8,128)}) %all-gather.3.cloned.1.call-update) | async-done | bytes 8388624 | tf_op jit(solution)/shard_map/all_gather | solution.py:26
  125.8 34.3 %while.14 = (s32[]{:T(128)}, f32[64,1024]{1,0:T(8,128)S(1)}, s32[]{:T(128)}, f32[32,64,1024]{2,1,0:T(8,128)}, s32[]{:T(128)}, /*index=5*/s32[]{:T(128)}) while((s32[]{:T(128)}, f32[64,1024]{1,0:T(8,128)S(1)}, s32[]{:T(128)}, f32[32,64,1024]{2,1,0:T(8,128)}, s32[]{:T(128)}, /*index=5*/s32[]{:T(128)}) %tuple.51), condition=%wide.region_6.7_spmd.clone, body=%wide.region_5.6_spmd.clone.sunk | while | flops 196612 | bytes 786525 | solution.py:34
  126.8 1.0 add_select_fusion.2
  127.9 1.0 add_select_fusion.2
  129.0 1.0 add_select_fusion.2
  136.5 1.0 add_select_fusion.2
  137.6 1.0 add_select_fusion.2
  156.8 1.0 add_select_fusion.2
  157.9 1.0 add_select_fusion.2
  161.1 114.4 %all-reduce.5.cloned.1.call-done = (f32[64,1024]{1,0:T(8,128)}, f32[3,64,1024]{2,1,0:T(8,128)}) async-done(((f32[64,1024]{1,0:T(8,128)}, f32[3,64,1024]{2,1,0:T(8,128)}), (f32[64,1024]{1,0:T(8,128)}, f32[3,64,1024]{2,1,0:T(8,128)})) %all-reduce.5.cloned.1.call-update) | async-done | bytes 1048592 | tf_op jit(solution)/shard_map/psum | solution.py:69
  276.5 2.2 pad_maximum_fusion.12
  (50 shorter events, 28.5 us)
Async XLA Ops:
  7.2 118.6 %all-gather.3.cloned.1.call-start = ((), (), s32[]{:S(2)}) async-start(), calls=%async_computation | async-start | bytes 8650752 | tf_op jit(solution)/shard_map/all_gather | solution.py:26
  8.3 7.9 %collective-permute-start.1 = (f32[1,64,1024]{2,1,0:T(8,128)S(1)}, f32[1,64,1024]{2,1,0:T(8,128)S(1)}, u32[]{:S(2)}, u32[]{:S(2)}) collective-permute-start(f32[1,64,1024]{2,1,0:T(8,128)S(1)} %get-tuple-element.119), channel_id=1, source_target_pairs={{0,8},{8,16},{16,24},{24,32},{32,40},{40,48},{48,56},{56,64},{64,7... | collective-permute-start | bytes 786440 | tf_op jit(solution)/shard_map/ppermute | solution.py:15
  12.9 7.7 %collective-permute-start = (f32[1,64,1024]{2,1,0:T(8,128)S(1)}, f32[1,64,1024]{2,1,0:T(8,128)S(1)}, u32[]{:S(2)}, u32[]{:S(2)}) collective-permute-start(f32[1,64,1024]{2,1,0:T(8,128)S(1)} %get-tuple-element.118), channel_id=1, source_target_pairs={{8,0},{16,8},{24,16},{32,24},{40,32},{48,40},{56,48},{64,56},{72,6... | collective-permute-start | bytes 786440 | tf_op jit(solution)/shard_map/ppermute | solution.py:17
  20.6 8.4 %copy-start.4 = (f32[8,64,1024]{2,1,0:T(8,128)S(1)}, f32[8,64,1024]{2,1,0:T(8,128)}, u32[]{:S(2)}) copy-start(f32[8,64,1024]{2,1,0:T(8,128)} %param.5) | copy-start | bytes 6291460
  20.7 5.9 %collective-permute-start.2 = (f32[10,1,1024]{2,1,0:T(1,128)S(1)}, f32[10,1,1024]{2,1,0:T(1,128)S(1)}, u32[]{:S(2)}, u32[]{:S(2)}) collective-permute-start(f32[10,1,1024]{2,1,0:T(1,128)S(1)} %get-tuple-element.115), channel_id=1, source_target_pairs={{1,0},{2,1},{3,2},{4,3},{5,4},{6,5},{7,6},{9,8},{10,9},{11,10},{12... | collective-permute-start | bytes 122888 | tf_op jit(solution)/shard_map/ppermute | solution.py:17
  22.1 6.9 %copy-start.1 = (f32[8,64,1024]{2,1,0:T(8,128)S(1)}, f32[8,64,1024]{2,1,0:T(8,128)}, u32[]{:S(2)}) copy-start(f32[8,64,1024]{2,1,0:T(8,128)} %param.6) | copy-start | bytes 6291460
  22.1 6.9 %copy-start.3 = (s32[8,64,1024]{2,1,0:T(8,128)S(1)}, s32[8,64,1024]{2,1,0:T(8,128)}, u32[]{:S(2)}) copy-start(s32[8,64,1024]{2,1,0:T(8,128)} %param.7) | copy-start | bytes 6291460
  22.1 5.5 %collective-permute-start.3 = (f32[10,1,1024]{2,1,0:T(1,128)S(1)}, f32[10,1,1024]{2,1,0:T(1,128)S(1)}, u32[]{:S(2)}, u32[]{:S(2)}) collective-permute-start(f32[10,1,1024]{2,1,0:T(1,128)S(1)} %get-tuple-element.114), channel_id=1, source_target_pairs={{0,1},{1,2},{2,3},{3,4},{4,5},{5,6},{6,7},{8,9},{9,10},{10,11},{11... | collective-permute-start | bytes 122888 | tf_op jit(solution)/shard_map/ppermute | solution.py:15
  31.5 18.8 %copy-start = (f32[8,64,1024]{2,1,0:T(8,128)}, f32[8,64,1024]{2,1,0:T(8,128)S(1)}, u32[]{:S(2)}) copy-start(f32[8,64,1024]{2,1,0:T(8,128)S(1)} %fusion.11) | copy-start | bytes 6291460
  31.5 7.7 %collective-permute-start.4 = (f32[1,64,1024]{2,1,0:T(8,128)S(1)}, f32[1,64,1024]{2,1,0:T(8,128)S(1)}, u32[]{:S(2)}, u32[]{:S(2)}) collective-permute-start(f32[1,64,1024]{2,1,0:T(8,128)S(1)} %get-tuple-element.117), channel_id=1, source_target_pairs={{8,0},{16,8},{24,16},{32,24},{40,32},{48,40},{56,48},{64,56},{72,6... | collective-permute-start | bytes 786440 | tf_op jit(solution)/shard_map/ppermute | solution.py:17
  33.5 6.9 %collective-permute-start.5 = (f32[1,64,1024]{2,1,0:T(8,128)S(1)}, f32[1,64,1024]{2,1,0:T(8,128)S(1)}, u32[]{:S(2)}, u32[]{:S(2)}) collective-permute-start(f32[1,64,1024]{2,1,0:T(8,128)S(1)} %get-tuple-element.116), channel_id=1, source_target_pairs={{0,8},{8,16},{16,24},{24,32},{32,40},{40,48},{48,56},{56,64},{64,7... | collective-permute-start | bytes 786440 | tf_op jit(solution)/shard_map/ppermute | solution.py:15
  40.5 5.6 %collective-permute-start.6 = (f32[10,1,1024]{2,1,0:T(1,128)S(1)}, f32[10,1,1024]{2,1,0:T(1,128)S(1)}, u32[]{:S(2)}, u32[]{:S(2)}) collective-permute-start(f32[10,1,1024]{2,1,0:T(1,128)S(1)} %get-tuple-element.113), channel_id=1, source_target_pairs={{1,0},{2,1},{3,2},{4,3},{5,4},{6,5},{7,6},{9,8},{10,9},{11,10},{12... | collective-permute-start | bytes 122888 | tf_op jit(solution)/shard_map/ppermute | solution.py:17
  41.8 5.4 %collective-permute-start.7 = (f32[10,1,1024]{2,1,0:T(1,128)S(1)}, f32[10,1,1024]{2,1,0:T(1,128)S(1)}, u32[]{:S(2)}, u32[]{:S(2)}) collective-permute-start(f32[10,1,1024]{2,1,0:T(1,128)S(1)} %get-tuple-element.112), channel_id=1, source_target_pairs={{0,1},{1,2},{2,3},{3,4},{4,5},{5,6},{6,7},{8,9},{9,10},{10,11},{11... | collective-permute-start | bytes 122888 | tf_op jit(solution)/shard_map/ppermute | solution.py:15
  52.6 3.7 %copy-start.2 = (f32[8,64,1024]{2,1,0:T(8,128)}, f32[8,64,1024]{2,1,0:T(8,128)S(1)}, u32[]{:S(2)}) copy-start(f32[8,64,1024]{2,1,0:T(8,128)S(1)} %fusion.4) | copy-start | bytes 6291460
  56.3 219.2 %all-reduce.5.cloned.1.call-start = ((), (), s32[]{:S(2)}) async-start(), calls=%async_computation.1 | async-start | bytes 2097152 | tf_op jit(solution)/shard_map/psum | solution.py:69
Sparse Core Ops, SparseCore 0:
  56.4 69.2 all-gather.2
  161.2 114.2 all-reduce.4
where the time goes:
time: 287 us; the launch traced here: 286 us
  waiting for transfers between devices  193 us (67%)
  other arithmetic  50.6 us (18%)
  starting transfers between devices  23.6 us (8%)
  between operations  14.3 us (5%)
  local copies, waits for them, and re-layouts  2.96 us (1%)
    psum x1, waiting for transfers between devices, shards(): shaded, total = lax.psum((attenuated, own_depth), 'depth')  114 us
    all_gather x1, waiting for transfers between devices, prefix(): everything = lax.all_gather(x, axis)  69.4 us
    select_n x32, other arithmetic, lap(): return jnp.where(reached, new, before)  33.5 us
    ppermute x4, starting transfers between devices, padded_2(): lax.ppermute(tail, axis, [(i, (i + 1) % count) for i in range(ends)])  17 us
    ppermute x4, starting transfers between devices, padded_2(): lax.ppermute(head, axis, [((i + 1) % count, i) for i in range(ends)])  6.56 us
  transfers between devices with their start and end apart: 10, of which 8 were waited for; matrix products, arithmetic and copies ran while one was open for 1% of the time, Pallas kernels for 0%

commit v1 on v0

v1 whole, which is shorter than its diff:
```python
import functools
import math

import jax
import jax.numpy as jnp
from jax import lax
from jax.experimental import pallas as pl
from jax.experimental.pallas import tpu as pltpu
from jax.sharding import PartitionSpec as P

MESH = pl.DeviceIdType.MESH
LANES = 128
ROWS = 8
SPREAD = 2


def leap(before, field, closed, p, r, l):
    lane = lax.broadcasted_iota(jnp.int32, (ROWS, LANES), 1)
    row = lax.broadcasted_iota(jnp.int32, (ROWS, LANES), 0)

    def tile(dp=0, dr=0, dl=0):
        return field[p + dp, pl.ds(pl.multiple_of(r + dr, ROWS), ROWS), pl.ds(pl.multiple_of(l + dl, LANES), LANES)]

    here = tile()
    west = pltpu.roll(jnp.where(lane == LANES - 1, tile(dl=-LANES), here), 1, 1)
    east = pltpu.roll(jnp.where(lane == 0, tile(dl=LANES), here), LANES - 1, 1)
    north = pltpu.roll(jnp.where(row == ROWS - 1, tile(dr=-ROWS), here), 1, 0)
    south = pltpu.roll(jnp.where(row == 0, tile(dr=ROWS), here), ROWS - 1, 0)
    beside = (tile(dp=-1) + tile(dp=1)) + ((north + south) + (west + east))
    ahead = (0.2 * here - before) + 0.3 * beside
    return jnp.where(closed == 0, ahead, 0.0)


def kernel(
    steps, now_h, old_h, flag_h, mid_h, new_h, image_h,
    now, old, flag, mid, new, part, peer, joint, shares, final, blue,
    load_sem, store_sem, face_send, face_recv, pair_send, pair_recv,
    share_send, share_recv, spread_send, spread_recv, swap_send, swap_recv,
):
    depth_count, tile_count = lax.axis_size("depth"), lax.axis_size("tile")
    d, t = lax.axis_index("depth"), lax.axis_index("tile")
    planes, rows, cols = now_h.shape
    blocks, tiles = rows // ROWS, cols // LANES
    chips = depth_count // 2
    core, chip = lax.rem(d, 2), lax.div(d, 2)
    half = blocks // 2
    d_up, d_down = lax.rem(d + 1, depth_count), lax.rem(d + depth_count - 1, depth_count)
    t_up, t_down = lax.rem(t + 1, tile_count), lax.rem(t + tile_count - 1, tile_count)
    partner = d + 1 - 2 * core
    inner_rows, inner_cols = pl.ds(ROWS, rows), pl.ds(LANES, cols)

    loads = [
        pltpu.make_async_copy(src, dst, load_sem.at[i])
        for i, (src, dst) in enumerate(
            (
                (now_h, now.at[pl.ds(1, planes), inner_rows, inner_cols]),
                (old_h, old),
                (flag_h, flag),
            )
        )
    ]
    for copy in loads:
        copy.start()

    barrier = pltpu.get_barrier_semaphore()
    for who in ((d_up, t), (d_down, t), (d, t_up), (d, t_down)):
        pl.semaphore_signal(barrier, inc=1, device_id=who, device_id_type=MESH)

    def greet(k, carry):
        other = lax.rem(chip + k, chips) * 2 + core
        pl.semaphore_signal(barrier, inc=1, device_id=(other, t), device_id_type=MESH)
        return carry

    lax.fori_loop(1, chips, greet, 0)
    pl.semaphore_wait(barrier, 4 + chips - 1)

    def faces(stage, low, high, first, last, field):
        ends = (
            (low, field.at[planes + 1, inner_rows, inner_cols], (d_down, t)),
            (high, field.at[0, inner_rows, inner_cols], (d_up, t)),
            (first, field.at[pl.ds(1, planes), pl.ds(ROWS + rows, ROWS), inner_cols], (d, t_down)),
            (last, field.at[pl.ds(1, planes), pl.ds(0, ROWS), inner_cols], (d, t_up)),
        )
        return [
            pltpu.make_async_remote_copy(
                src_ref=src,
                dst_ref=dst,
                send_sem=face_send.at[stage, i],
                recv_sem=face_recv.at[stage, i],
                device_id=who,
                device_id_type=MESH,
            )
            for i, (src, dst, who) in enumerate(ends)
        ]

    def clear_edges(field):
        @pl.when(d == 0)
        def _():
            field[0, inner_rows, inner_cols] = jnp.zeros((rows, cols), jnp.float32)

        @pl.when(d == depth_count - 1)
        def _():
            field[planes + 1, inner_rows, inner_cols] = jnp.zeros((rows, cols), jnp.float32)

        @pl.when(t == 0)
        def _():
            field[pl.ds(1, planes), pl.ds(0, ROWS), inner_cols] = jnp.zeros((planes, ROWS, cols), jnp.float32)

        @pl.when(t == tile_count - 1)
        def _():
            field[pl.ds(1, planes), pl.ds(ROWS + rows, ROWS), inner_cols] = jnp.zeros((planes, ROWS, cols), jnp.float32)

    now_faces = faces(
        0,
        now_h.at[0],
        now_h.at[planes - 1],
        now_h.at[:, pl.ds(0, ROWS)],
        now_h.at[:, pl.ds(rows - ROWS, ROWS)],
        now,
    )
    for copy in now_faces:
        copy.start()

    for field in (now, mid):
        for side in (0, LANES + cols):
            field[pl.ds(1, planes), inner_rows, pl.ds(side, LANES)] = jnp.zeros((planes, rows, LANES), jnp.float32)
    for copy in loads:
        copy.wait()

    def over(count, body):
        turns = tiles // SPREAD

        def lap(n, carry):
            i, j = lax.div(n, turns), lax.rem(n, turns)
            for s in range(SPREAD):
                body(i, pl.multiple_of((j * SPREAD + s) * LANES, LANES))
            return carry

        lax.fori_loop(0, count * turns, lap, 0)

    def mid_tile(p, b, l):
        r = pl.multiple_of(b * ROWS, ROWS)
        here = (pl.ds(r, ROWS), pl.ds(l, LANES))
        mid[p + 1, pl.ds(pl.multiple_of(r + ROWS, ROWS), ROWS), pl.ds(pl.multiple_of(l + LANES, LANES), LANES)] = leap(
            old[(p,) + here], now, flag[(p,) + here], p + 1, r + ROWS, l + LANES
        )

    def mid_inner(i, l):
        for p in range(1, planes - 1):
            mid_tile(p, i + 1, l)

    def mid_outer(i, l):
        for p in (0, planes - 1):
            mid_tile(p, i, l)

    def mid_rows(i, l):
        for p in range(1, planes - 1):
            mid_tile(p, i * (blocks - 1), l)

    over(blocks - 2, mid_inner)
    for copy in now_faces:
        copy.wait_recv()
    clear_edges(now)
    over(blocks, mid_outer)
    mid_faces = faces(
        1,
        mid.at[1, inner_rows, inner_cols],
        mid.at[planes, inner_rows, inner_cols],
        mid.at[pl.ds(1, planes), pl.ds(ROWS, ROWS), inner_cols],
        mid.at[pl.ds(1, planes), pl.ds(rows, ROWS), inner_cols],
        mid,
    )
    mid_faces[0].start()
    mid_faces[1].start()
    over(2, mid_rows)
    mid_faces[2].start()
    mid_faces[3].start()
    mid_store = pltpu.make_async_copy(mid.at[pl.ds(1, planes), inner_rows, inner_cols], mid_h, store_sem.at[0])
    mid_store.start()

    rate = steps * math.log2(math.e)

    def new_tile(p, b, l):
        r = pl.multiple_of(b * ROWS, ROWS)
        here = (pl.ds(r, ROWS), pl.ds(l, LANES))
        before = now[p + 1, pl.ds(pl.multiple_of(r + ROWS, ROWS), ROWS), pl.ds(pl.multiple_of(l + LANES, LANES), LANES)]
        value = leap(before, mid, flag[(p,) + here], p + 1, r + ROWS, l + LANES)
        new[(p,) + here] = value
        square = value * value
        thick = square * pltpu.reciprocal(1.0 + square, approx=True)
        return thick, jnp.tanh(1.5 * value), jnp.exp2((-0.5 * math.log2(math.e)) * square)

    def place(b, l):
        return (pl.ds(pl.multiple_of(b * ROWS, ROWS), ROWS), pl.ds(l, LANES))

    def inner(b, l):
        at = place(b, l)
        depth = light = red = green = None
        for p in range(1, planes - 1):
            thick, warm, mild = new_tile(p, b, l)
            if depth is None:
                depth = thick
                after = jnp.exp2(-rate * depth)
                weight = 1.0 - after
                red, green = weight * warm, weight * mild
            else:
                depth = depth + thick
                after = jnp.exp2(-rate * depth)
                weight = light - after
                red, green = red + weight * warm, green + weight * mild
            light = after
        part[(0,) + at], part[(1,) + at], part[(2,) + at] = red, green, depth

    def outer(b, l):
        at = place(b, l)
        depth = part[(2,) + at]
        thick_a, warm_a, mild_a = new_tile(0, b, l)
        thick_b, warm_b, mild_b = new_tile(planes - 1, b, l)
        light_a = jnp.exp2(-rate * thick_a)
        depth_b = thick_a + depth
        light_b = jnp.exp2(-rate * depth_b)
        depth_c = depth_b + thick_b
        light_c = jnp.exp2(-rate * depth_c)
        weight_a, weight_b = 1.0 - light_a, light_b - light_c
        part[(0,) + at] = weight_a * warm_a + light_a * part[(0,) + at] + weight_b * warm_b
        part[(1,) + at] = weight_a * mild_a + light_a * part[(1,) + at] + weight_b * mild_b
        part[(2,) + at] = depth_c

    over(blocks - 2, lambda i, l: inner(i + 1, l))
    for copy in mid_faces:
        copy.wait_recv()
    clear_edges(mid)
    over(2, lambda i, l: inner(i * (blocks - 1), l))

    def pair(i):
        mine = pl.ds(pl.multiple_of(((1 - core) * half + i) * ROWS, ROWS), ROWS)
        theirs = pl.ds(pl.multiple_of(i * ROWS, ROWS), ROWS)
        return pltpu.make_async_remote_copy(
            src_ref=part.at[:, mine],
            dst_ref=peer.at[:, theirs],
            send_sem=pair_send.at[i],
            recv_sem=pair_recv.at[i],
            device_id=(partner, t),
            device_id_type=MESH,
        )

    def give(i, carry):
        over(1, lambda _, l: outer((1 - core) * half + i, l))
        pair(i).start()
        return carry

    lax.fori_loop(0, half, give, 0)

    def share(i, j, who):
        return pltpu.make_async_remote_copy(
            src_ref=joint.at[:, pl.ds(pl.multiple_of(i * ROWS, ROWS), ROWS), pl.ds(pl.multiple_of(j * LANES, LANES), LANES)],
            dst_ref=shares.at[lax.div(i, 2), chip],
            send_sem=share_send.at[lax.div(i, 2), who],
            recv_sem=share_recv.at[lax.div(i, 2), chip],
            device_id=(who * 2 + core, t),
            device_id_type=MESH,
        )

    def join(i, carry):
        over(1, lambda _, l: outer(core * half + i, l))
        pair(i).wait_recv()

        def merge(_, l):
            mine, theirs = place(core * half + i, l), place(i, l)
            first = core == 0
            own = [part[(c,) + mine] for c in range(3)]
            other = [peer[(c,) + theirs] for c in range(3)]
            light = jnp.exp2(-rate * jnp.where(first, own[2], other[2]))
            for c in range(2):
                joint[(c,) + theirs] = jnp.where(first, own[c], other[c]) + light * jnp.where(first, other[c], own[c])
            joint[(2,) + theirs] = own[2] + other[2]

        over(1, merge)

        def send(k, carry):
            j = lax.rem(k + chip, tiles)
            who = lax.rem(i, 2) * tiles + j

            @pl.when(who != chip)
            def _():
                share(i, j, who).start()

            @pl.when(who == chip)
            def _():
                at = place(i, pl.multiple_of(j * LANES, LANES))
                for c in range(3):
                    shares[lax.div(i, 2), chip, c] = joint[(c,) + at]

            return carry

        return lax.fori_loop(0, tiles, send, carry)

    lax.fori_loop(0, half, join, 0)
    new_store = pltpu.make_async_copy(new, new_h, store_sem.at[1])
    new_store.start()

    def spread(s, who):
        i = 2 * s + lax.div(chip, tiles)
        at = final.at[
            :,
            pl.ds(pl.multiple_of((core * half + i) * ROWS, ROWS), ROWS),
            pl.ds(pl.multiple_of(lax.rem(chip, tiles) * LANES, LANES), LANES),
        ]
        return pltpu.make_async_remote_copy(
            src_ref=at,
            dst_ref=at,
            send_sem=spread_send.at[s, who],
            recv_sem=spread_recv.at[s, chip],
            device_id=(who * 2 + core, t),
            device_id_type=MESH,
        )

    def spread_in(s, whose):
        i = 2 * s + lax.div(whose, tiles)
        at = final.at[
            :,
            pl.ds(pl.multiple_of((core * half + i) * ROWS, ROWS), ROWS),
            pl.ds(pl.multiple_of(lax.rem(whose, tiles) * LANES, LANES), LANES),
        ]
        return pltpu.make_async_copy(at, at, spread_recv.at[s, whose])

    def others(body):
        def one(k, carry):
            body(lax.rem(chip + k, chips))
            return carry

        lax.fori_loop(1, chips, one, 0)

    for s in range(2):
        others(lambda who: pltpu.make_async_copy(shares.at[s, who], shares.at[s, who], share_recv.at[s, who]).wait())

        def compose(k, carry):
            red, green, depth = carry
            light = jnp.exp2(-rate * depth)
            return (
                red + light * shares[s, k, 0],
                green + light * shares[s, k, 1],
                depth + shares[s, k, 2],
            )

        zero = jnp.zeros((ROWS, LANES), jnp.float32)
        red, green, depth = lax.fori_loop(0, chips, compose, (zero, zero, zero))
        opacity = 1.0 - jnp.exp2(-rate * depth)
        at = place(
            core * half + 2 * s + lax.div(chip, tiles), pl.multiple_of(lax.rem(chip, tiles) * LANES, LANES)
        )
        final[(0,) + at], final[(1,) + at], final[(2,) + at] = 0.5 * (opacity + red), green, opacity
        others(lambda who: spread(s, who).start())

    def swap(s, whose):
        at = final.at[:, pl.ds(pl.multiple_of((whose * half + 2 * s) * ROWS, ROWS), 2 * ROWS)]
        return pltpu.make_async_remote_copy(
            src_ref=at,
            dst_ref=at,
            send_sem=swap_send.at[s],
            recv_sem=swap_recv.at[s],
            device_id=(partner, t),
            device_id_type=MESH,
        )

    for s in range(2):
        others(lambda who: spread_in(s, who).wait())
        swap(s, core).start()
    for s in range(2):
        swap(s, 1 - core).wait_recv()
    blue[...] = final[2] - final[0]
    image_stores = [
        pltpu.make_async_copy(src, image_h.at[c], store_sem.at[2 + c])
        for c, src in enumerate((final.at[0], final.at[1], blue, final.at[2]))
    ]
    for copy in image_stores:
        copy.start()

    for copy in now_faces + mid_faces:
        copy.wait_send()

    def drain(i, carry):
        pair(i).wait_send()
        return carry

    lax.fori_loop(0, half, drain, 0)
    for s in range(2):
        others(lambda who: pltpu.make_async_copy(shares.at[s, who], shares.at[s, who], share_send.at[s, who]).wait())
        others(lambda who: spread(s, who).wait_send())
        swap(s, core).wait_send()
    mid_store.wait()
    new_store.wait()
    for copy in image_stores:
        copy.wait()


def shards(pressure_old, pressure_now, solid_flags):
    planes, rows, cols = pressure_now.shape
    chips = lax.axis_size("depth") // 2
    half = rows // 2
    any_space = pl.BlockSpec(memory_space=pl.ANY)
    f32 = jnp.float32
    halo = (planes + 2, rows + 2 * ROWS, cols + 2 * LANES)
    return pl.pallas_call(
        functools.partial(kernel, 4.0 / (planes * lax.axis_size("depth"))),
        out_shape=[
            jax.ShapeDtypeStruct(pressure_now.shape, f32),
            jax.ShapeDtypeStruct(pressure_now.shape, f32),
            jax.ShapeDtypeStruct((4, rows, cols), f32),
        ],
        in_specs=[any_space] * 3,
        out_specs=[any_space] * 3,
        scratch_shapes=[
            pltpu.VMEM(halo, f32),
            pltpu.VMEM(pressure_now.shape, f32),
            pltpu.VMEM(pressure_now.shape, jnp.int32),
            pltpu.VMEM(halo, f32),
            pltpu.VMEM(pressure_now.shape, f32),
            pltpu.VMEM((3, rows, cols), f32),
            pltpu.VMEM((3, half, cols), f32),
            pltpu.VMEM((3, half, cols), f32),
            pltpu.VMEM((2, chips, 3, ROWS, LANES), f32),
            pltpu.VMEM((3, rows, cols), f32),
            pltpu.VMEM((rows, cols), f32),
            pltpu.SemaphoreType.DMA((3,)),
            pltpu.SemaphoreType.DMA((6,)),
            pltpu.SemaphoreType.DMA((2, 4)),
            pltpu.SemaphoreType.DMA((2, 4)),
            pltpu.SemaphoreType.DMA((half // ROWS,)),
            pltpu.SemaphoreType.DMA((half // ROWS,)),
            pltpu.SemaphoreType.DMA((2, chips)),
            pltpu.SemaphoreType.DMA((2, chips)),
            pltpu.SemaphoreType.DMA((2, chips)),
            pltpu.SemaphoreType.DMA((2, chips)),
            pltpu.SemaphoreType.DMA((2,)),
            pltpu.SemaphoreType.DMA((2,)),
        ],
        compiler_params=pltpu.CompilerParams(
            collective_id=0, has_side_effects=True, vmem_limit_bytes=48 * 1024 * 1024
        ),
    )(pressure_now, pressure_old, solid_flags)


def solution(mesh):
    return jax.shard_map(
        shards,
        mesh=mesh,
        in_specs=(P("depth", "tile", None), P("depth", "tile", None), P("depth", "tile", None)),
        out_specs=(P("depth", "tile", None), P("depth", "tile", None), P(None, "tile", None)),
        check_vma=False,
    )
```

time: 287 us -> 55.2 us (0.19)
  waiting for transfers between devices: 193 us -> 0 us
  Pallas kernels: 0 us -> 50.9 us
  other arithmetic: 50.6 us -> 0 us
  starting transfers between devices: 23.6 us -> 0 us
  between operations: 14.3 us -> 0.64 us
    psum x1 -> x0, waiting for transfers between devices: 114 us -> none  [shards(): shaded, total = lax.psum((attenuated, own_depth), 'depth')]
    all_gather x1 -> x0, waiting for transfers between devices: 69.4 us -> none  [prefix(): everything = lax.all_gather(x, axis)]
    pallas_call x0 -> x1, Pallas kernels: none -> 50.9 us  [shards(): pl.pallas_call(functools.partial(kernel, 4.0 / (planes * lax.axis_size('d...]
    select_n x32 -> x0, other arithmetic: 33.5 us -> none  [lap(): return jnp.where(reached, new, before)]
    ppermute x8 -> x0, starting transfers between devices: 23.5 us -> none  [the longest x4 17 us: padded_2(): lax.ppermute(tail, axis, [(i, (i + 1) % count) for i in range(ends)])]
    ppermute x8 -> x0, waiting for transfers between devices: 9.44 us -> none  [the longest x4 4.76 us: padded_2(): lax.ppermute(head, axis, [((i + 1) % count, i) for i in range(ends)])]
    concatenate x4 -> x0, other arithmetic: 6.65 us -> none  [the longest x3 4.44 us: padded_2(): jnp.concatenate([lax.ppermute(tail, axis, [(i, (i + 1) % count) for i in...]
    mul x3 -> x0, other arithmetic: 5.79 us -> none  [the longest x2 4.83 us: advance(): open_field * (2.0 * current - previous + 0.3 * (beside - 6.0 * current))]
  transfers between devices with their start and end apart: 10 -> 0, of which waited for: 8 -> 0; matrix products, arithmetic and copies ran while one was open for 1% -> 0% of each run, Pallas kernels for 0% -> 0%
where the time goes in v1:
time: 55.2 us; the launch traced here: 55.1 us
  Pallas kernels  50.9 us (92%)
  local copies, waits for them, and re-layouts  3.61 us (7%)
  between operations  0.64 us (1%)
    pallas_call x1, Pallas kernels, shards(): pl.pallas_call(functools.partial(kernel, 4.0 / (planes * lax.axis_size('d...  50.9 us
    unnamed x3, local copies, waits for them, and re-layouts  3.61 us

profile of v1, /device:TPU:1, one launch (start us, length us, event | category | flops | bytes accessed | tf_op | source)
XLA Modules:
  0.0 55.1 jit_solution(11319886934860407838)
XLA Ops:
  0.6 50.9 %shard_map.58 = (f32[8,64,1024]{2,1,0:T(8,128)S(1)}, f32[8,64,1024]{2,1,0:T(8,128)S(1)}, f32[4,64,1024]{2,1,0:T(8,128)S(1)}) custom-call(f32[8,64,1024]{2,1,0:T(8,128)} %now_h.1, f32[8,64,1024]{2,1,0:T(8,128)} %old_h.1, s32[8,64,1024]{2,1,0:T(8,128)} %flag_h.1), custom_call_target="tpu_custom_call" | custom-call | tf_op jit(solution)/shard_map/pallas_call | solution.py:404
  51.5 1.3 %copy.9 = f32[8,64,1024]{2,1,0:T(8,128)} copy(f32[8,64,1024]{2,1,0:T(8,128)S(1)} %get-tuple-element.6) | data formatting | bytes 4194304
  52.8 1.3 %copy.10 = f32[8,64,1024]{2,1,0:T(8,128)} copy(f32[8,64,1024]{2,1,0:T(8,128)S(1)} %get-tuple-element.7) | data formatting | bytes 4194304
  54.1 1.0 %copy.11 = f32[4,64,1024]{2,1,0:T(8,128)} copy(f32[4,64,1024]{2,1,0:T(8,128)S(1)} %get-tuple-element.8) | data formatting | bytes 2097152

commit v2 on v1

v2 whole, which is shorter than its diff:
```python
import functools
import math

import jax
import jax.numpy as jnp
from jax import lax
from jax.experimental import pallas as pl
from jax.experimental.pallas import tpu as pltpu
from jax.sharding import PartitionSpec as P

MESH = pl.DeviceIdType.MESH
LANES = 128
ROWS = 8
SPREAD = 8
PIECES = 4


def leap(before, field, closed, p, r, l):
    lane = lax.broadcasted_iota(jnp.int32, (ROWS, LANES), 1)
    row = lax.broadcasted_iota(jnp.int32, (ROWS, LANES), 0)

    def tile(dp=0, dr=0, dl=0):
        return field[p + dp, pl.ds(pl.multiple_of(r + dr, ROWS), ROWS), pl.ds(pl.multiple_of(l + dl, LANES), LANES)]

    here = tile()
    west = pltpu.roll(jnp.where(lane == LANES - 1, tile(dl=-LANES), here), 1, 1)
    east = pltpu.roll(jnp.where(lane == 0, tile(dl=LANES), here), LANES - 1, 1)
    north = pltpu.roll(jnp.where(row == ROWS - 1, tile(dr=-ROWS), here), 1, 0)
    south = pltpu.roll(jnp.where(row == 0, tile(dr=ROWS), here), ROWS - 1, 0)
    beside = (tile(dp=-1) + tile(dp=1)) + ((north + south) + (west + east))
    ahead = (0.2 * here - before) + 0.3 * beside
    return jnp.where(closed == 0, ahead, 0.0)


def kernel(
    steps, now_h, old_h, flag_h, mid_h, new_h, image_h,
    now, old, flag, mid, new, part, peer, joint, shares, final, blue,
    load_sem, store_sem, face_send, face_recv, edge_send, edge_recv, pair_send, pair_recv,
    share_send, share_recv, spread_send, spread_recv, swap_send, swap_recv,
):
    depth_count, tile_count = lax.axis_size("depth"), lax.axis_size("tile")
    d, t = lax.axis_index("depth"), lax.axis_index("tile")
    planes, rows, cols = now_h.shape
    blocks, tiles = rows // ROWS, cols // LANES
    chips = depth_count // 2
    core, chip = lax.rem(d, 2), lax.div(d, 2)
    piece = rows // PIECES
    d_up, d_down = lax.rem(d + 1, depth_count), lax.rem(d + depth_count - 1, depth_count)
    t_up, t_down = lax.rem(t + 1, tile_count), lax.rem(t + tile_count - 1, tile_count)
    has_d_up, has_d_down = d < depth_count - 1, d > 0
    has_t_up, has_t_down = t < tile_count - 1, t > 0
    partner = d + 1 - 2 * core
    inner_rows, inner_cols = pl.ds(ROWS, rows), pl.ds(LANES, cols)
    near = (
        (has_d_up, (d_up, t)),
        (has_d_down, (d_down, t)),
        (has_t_up, (d, t_up)),
        (has_t_down, (d, t_down)),
    )

    barrier = pltpu.get_barrier_semaphore()
    for there, who in near:

        @pl.when(there)
        def _():
            pl.semaphore_signal(barrier, inc=1, device_id=who, device_id_type=MESH)

    def greet(k, carry):
        other = lax.rem(chip + k, chips) * 2 + core
        pl.semaphore_signal(barrier, inc=1, device_id=(other, t), device_id_type=MESH)
        return carry

    lax.fori_loop(1, chips, greet, 0)

    loads = [
        pltpu.make_async_copy(src, dst, load_sem.at[i])
        for i, (src, dst) in enumerate(
            (
                (now_h, now.at[pl.ds(1, planes), inner_rows, inner_cols]),
                (old_h, old),
                (flag_h, flag),
            )
        )
    ]
    for copy in loads:
        copy.start()
    for field in (now, mid):
        for side in (0, LANES + cols):
            field[pl.ds(1, planes), inner_rows, pl.ds(side, LANES)] = jnp.zeros((planes, rows, LANES), jnp.float32)

        @pl.when(jnp.logical_not(has_d_down))
        def _():
            field[0, inner_rows, inner_cols] = jnp.zeros((rows, cols), jnp.float32)

        @pl.when(jnp.logical_not(has_d_up))
        def _():
            field[planes + 1, inner_rows, inner_cols] = jnp.zeros((rows, cols), jnp.float32)

        @pl.when(jnp.logical_not(has_t_down))
        def _():
            field[pl.ds(1, planes), pl.ds(0, ROWS), inner_cols] = jnp.zeros((planes, ROWS, cols), jnp.float32)

        @pl.when(jnp.logical_not(has_t_up))
        def _():
            field[pl.ds(1, planes), pl.ds(ROWS + rows, ROWS), inner_cols] = jnp.zeros((planes, ROWS, cols), jnp.float32)

    count = chips - 1
    for left in (d, depth_count - 1 - d, t, tile_count - 1 - t):
        count = count + jnp.minimum(left, 1)
    pl.semaphore_wait(barrier, count)

    def depth_face(stage, way, q):
        plane = (planes - 1) * way
        if stage == 0:
            src, field = now_h.at[plane, pl.ds(q * piece, piece)], now
        else:
            src, field = mid.at[plane + 1, pl.ds(ROWS + q * piece, piece), inner_cols], mid
        return pltpu.make_async_remote_copy(
            src_ref=src,
            dst_ref=field.at[(planes + 1) * (1 - way), pl.ds(ROWS + q * piece, piece), inner_cols],
            send_sem=face_send.at[stage, way, q],
            recv_sem=face_recv.at[stage, way, q],
            device_id=((d_down, d_up)[way], t),
            device_id_type=MESH,
        )

    def tile_face(stage, way):
        row = (rows - 1) * way
        if stage == 0:
            src, field = now_h.at[:, pl.ds(row, 1)], now
        else:
            src, field = mid.at[pl.ds(1, planes), pl.ds(ROWS + row, 1), inner_cols], mid
        return pltpu.make_async_remote_copy(
            src_ref=src,
            dst_ref=field.at[pl.ds(1, planes), pl.ds(ROWS + rows if way == 0 else ROWS - 1, 1), inner_cols],
            send_sem=edge_send.at[stage, way],
            recv_sem=edge_recv.at[stage, way],
            device_id=(d, (t_down, t_up)[way]),
            device_id_type=MESH,
        )

    d_to, t_to = (has_d_down, has_d_up), (has_t_down, has_t_up)
    d_from, t_from = d_to[::-1], t_to[::-1]

    def start_depth(stage, q):
        for way in range(2):
            pl.when(d_to[way])(lambda: depth_face(stage, way, q).start())

    def start_tile(stage, way):
        pl.when(t_to[way])(lambda: tile_face(stage, way).start())

    def await_depth(stage, q):
        for way in range(2):
            pl.when(d_from[way])(lambda: depth_face(stage, way, q).wait_recv())

    def await_tile(stage, way):
        pl.when(t_from[way])(lambda: tile_face(stage, way).wait_recv())

    for way in range(2):
        start_tile(0, way)
    for q in range(PIECES):
        start_depth(0, q)

    for copy in loads:
        copy.wait()

    def over(count, body):
        turns = tiles // SPREAD

        def lap(n, carry):
            i, j = lax.div(n, turns), lax.rem(n, turns)
            for s in range(SPREAD):
                body(i, pl.multiple_of((j * SPREAD + s) * LANES, LANES))
            return carry

        lax.fori_loop(0, count * turns, lap, 0)

    def mid_tile(p, b, l):
        r = pl.multiple_of(b * ROWS, ROWS)
        here = (pl.ds(r, ROWS), pl.ds(l, LANES))
        mid[p + 1, pl.ds(pl.multiple_of(r + ROWS, ROWS), ROWS), pl.ds(pl.multiple_of(l + LANES, LANES), LANES)] = leap(
            old[(p,) + here], now, flag[(p,) + here], p + 1, r + ROWS, l + LANES
        )

    def mid_inner(b, l):
        for p in range(1, planes - 1):
            mid_tile(p, b, l)

    def mid_outer(b, l):
        for p in (0, planes - 1):
            mid_tile(p, b, l)

    over(blocks - 2, lambda i, l: mid_inner(i + 1, l))
    for way in range(2):
        await_tile(0, way)
    over(2, lambda i, l: mid_inner(i * (blocks - 1), l))
    per = blocks // PIECES
    for q in range(PIECES):
        await_depth(0, q)
        over(per, lambda i, l: mid_outer(q * per + i, l))
        start_depth(1, q)
        if q == 0:
            start_tile(1, 0)
    start_tile(1, 1)
    mid_store = pltpu.make_async_copy(mid.at[pl.ds(1, planes), inner_rows, inner_cols], mid_h, store_sem.at[0])
    mid_store.start()

    rate = steps * math.log2(math.e)

    def new_tile(p, b, l):
        r = pl.multiple_of(b * ROWS, ROWS)
        here = (pl.ds(r, ROWS), pl.ds(l, LANES))
        before = now[p + 1, pl.ds(pl.multiple_of(r + ROWS, ROWS), ROWS), pl.ds(pl.multiple_of(l + LANES, LANES), LANES)]
        value = leap(before, mid, flag[(p,) + here], p + 1, r + ROWS, l + LANES)
        new[(p,) + here] = value
        square = value * value
        thick = square * pltpu.reciprocal(1.0 + square, approx=True)
        return thick, jnp.tanh(1.5 * value), jnp.exp2((-0.5 * math.log2(math.e)) * square)

    def place(b, l):
        return (pl.ds(pl.multiple_of(b * ROWS, ROWS), ROWS), pl.ds(l, LANES))

    def inner(b, l):
        at = place(b, l)
        depth = light = red = green = None
        for p in range(1, planes - 1):
            thick, warm, mild = new_tile(p, b, l)
            if depth is None:
                depth = thick
                after = jnp.exp2(-rate * depth)
                weight = 1.0 - after
                red, green = weight * warm, weight * mild
            else:
                depth = depth + thick
                after = jnp.exp2(-rate * depth)
                weight = light - after
                red, green = red + weight * warm, green + weight * mild
            light = after
        part[(0,) + at], part[(1,) + at], part[(2,) + at] = red, green, depth

    def outer(b, l):
        at = place(b, l)
        depth = part[(2,) + at]
        thick_a, warm_a, mild_a = new_tile(0, b, l)
        thick_b, warm_b, mild_b = new_tile(planes - 1, b, l)
        light_a = jnp.exp2(-rate * thick_a)
        depth_b = thick_a + depth
        light_b = jnp.exp2(-rate * depth_b)
        depth_c = depth_b + thick_b
        light_c = jnp.exp2(-rate * depth_c)
        weight_a, weight_b = 1.0 - light_a, light_b - light_c
        part[(0,) + at] = weight_a * warm_a + light_a * part[(0,) + at] + weight_b * warm_b
        part[(1,) + at] = weight_a * mild_a + light_a * part[(1,) + at] + weight_b * mild_b
        part[(2,) + at] = depth_c

    def joined(s, whose):
        return 4 * s + 2 * whose

    def pair(s):
        return pltpu.make_async_remote_copy(
            src_ref=part.at[:, pl.ds(pl.multiple_of(joined(s, 1 - core) * ROWS, ROWS), 2 * ROWS)],
            dst_ref=peer.at[s],
            send_sem=pair_send.at[s],
            recv_sem=pair_recv.at[s],
            device_id=(partner, t),
            device_id_type=MESH,
        )

    def share(s, n, who):
        i, j = lax.div(n, tiles), lax.rem(n, tiles)
        return pltpu.make_async_remote_copy(
            src_ref=joint.at[s, :, pl.ds(pl.multiple_of(i * ROWS, ROWS), ROWS), pl.ds(pl.multiple_of(j * LANES, LANES), LANES)],
            dst_ref=shares.at[s, chip],
            send_sem=share_send.at[s, who],
            recv_sem=share_recv.at[s, chip],
            device_id=(who * 2 + core, t),
            device_id_type=MESH,
        )

    def others(body):
        def one(k, carry):
            body(lax.rem(chip + k, chips))
            return carry

        lax.fori_loop(1, chips, one, 0)

    over(blocks - 2, lambda i, l: inner(i + 1, l))
    for s in range(2):
        await_tile(1, 1 - s)
        over(1, lambda _, l: inner(s * (blocks - 1), l))
        for q in range(s * PIECES // 2, (s + 1) * PIECES // 2):
            await_depth(1, q)
        over(2, lambda i, l: outer(joined(s, 1 - core) + i, l))
        pair(s).start()
        over(2, lambda i, l: outer(joined(s, core) + i, l))
        if s == 1:
            new_store = pltpu.make_async_copy(new, new_h, store_sem.at[1])
            new_store.start()
        pair(s).wait_recv()

        def merge(i, l):
            mine, theirs = place(joined(s, core) + i, l), place(i, l)
            first = core == 0
            own = [part[(c,) + mine] for c in range(3)]
            other = [peer[(s, c) + theirs] for c in range(3)]
            light = jnp.exp2(-rate * jnp.where(first, own[2], other[2]))
            for c in range(2):
                joint[(s, c) + theirs] = jnp.where(first, own[c], other[c]) + light * jnp.where(first, other[c], own[c])
            joint[(s, 2) + theirs] = own[2] + other[2]

        over(2, merge)
        others(lambda who: share(s, who, who).start())
        own_tile = place(lax.div(chip, tiles), pl.multiple_of(lax.rem(chip, tiles) * LANES, LANES))
        for c in range(3):
            shares[s, chip, c] = joint[(s, c) + own_tile]

    def region(s, whose):
        at = place(
            joined(s, core) + lax.div(whose, tiles), pl.multiple_of(lax.rem(whose, tiles) * LANES, LANES)
        )
        return final.at[(slice(None),) + at]

    def spread(s, who):
        return pltpu.make_async_remote_copy(
            src_ref=region(s, chip),
            dst_ref=region(s, chip),
            send_sem=spread_send.at[s, who],
            recv_sem=spread_recv.at[s, chip],
            device_id=(who * 2 + core, t),
            device_id_type=MESH,
        )

    def swap(s, whose):
        at = final.at[:, pl.ds(pl.multiple_of(joined(s, whose) * ROWS, ROWS), 2 * ROWS)]
        return pltpu.make_async_remote_copy(
            src_ref=at,
            dst_ref=at,
            send_sem=swap_send.at[s],
            recv_sem=swap_recv.at[s],
            device_id=(partner, t),
            device_id_type=MESH,
        )

    for s in range(2):
        others(lambda who: pltpu.make_async_copy(shares.at[s, who], shares.at[s, who], share_recv.at[s, who]).wait())

        def compose(k, carry):
            red, green, depth = carry
            light = jnp.exp2(-rate * depth)
            return (
                red + light * shares[s, k, 0],
                green + light * shares[s, k, 1],
                depth + shares[s, k, 2],
            )

        zero = jnp.zeros((ROWS, LANES), jnp.float32)
        red, green, depth = lax.fori_loop(0, chips, compose, (zero, zero, zero))
        opacity = 1.0 - jnp.exp2(-rate * depth)
        at = place(
            joined(s, core) + lax.div(chip, tiles), pl.multiple_of(lax.rem(chip, tiles) * LANES, LANES)
        )
        final[(0,) + at], final[(1,) + at], final[(2,) + at] = 0.5 * (opacity + red), green, opacity
        others(lambda who: spread(s, who).start())

    image_stores = []
    for s in range(2):
        others(lambda who: pltpu.make_async_copy(region(s, who), region(s, who), spread_recv.at[s, who]).wait())
        swap(s, core).start()
    for s in range(2):
        swap(s, 1 - core).wait_recv()
        half = pl.ds(s * rows // 2, rows // 2)
        blue[half] = final[2, half] - final[0, half]
        for c, src in enumerate((final.at[0, half], final.at[1, half], blue.at[half], final.at[2, half])):
            copy = pltpu.make_async_copy(src, image_h.at[c, half], store_sem.at[2 + 4 * s + c])
            copy.start()
            image_stores.append(copy)

    for stage in range(2):
        for way in range(2):
            for q in range(PIECES):
                pl.when(d_to[way])(lambda: depth_face(stage, way, q).wait_send())
            pl.when(t_to[way])(lambda: tile_face(stage, way).wait_send())
    for s in range(2):
        pair(s).wait_send()
        others(lambda who: share(s, who, who).wait_send())
        others(lambda who: spread(s, who).wait_send())
        swap(s, core).wait_send()
    mid_store.wait()
    new_store.wait()
    for copy in image_stores:
        copy.wait()


def shards(pressure_old, pressure_now, solid_flags):
    planes, rows, cols = pressure_now.shape
    chips = lax.axis_size("depth") // 2
    any_space = pl.BlockSpec(memory_space=pl.ANY)
    f32 = jnp.float32
    halo = (planes + 2, rows + 2 * ROWS, cols + 2 * LANES)
    return pl.pallas_call(
        functools.partial(kernel, 4.0 / (planes * lax.axis_size("depth"))),
        out_shape=[
            jax.ShapeDtypeStruct(pressure_now.shape, f32),
            jax.ShapeDtypeStruct(pressure_now.shape, f32),
            jax.ShapeDtypeStruct((4, rows, cols), f32),
        ],
        in_specs=[any_space] * 3,
        out_specs=[any_space] * 3,
        scratch_shapes=[
            pltpu.VMEM(halo, f32),
            pltpu.VMEM(pressure_now.shape, f32),
            pltpu.VMEM(pressure_now.shape, jnp.int32),
            pltpu.VMEM(halo, f32),
            pltpu.VMEM(pressure_now.shape, f32),
            pltpu.VMEM((3, rows, cols), f32),
            pltpu.VMEM((2, 3, 2 * ROWS, cols), f32),
            pltpu.VMEM((2, 3, 2 * ROWS, cols), f32),
            pltpu.VMEM((2, chips, 3, ROWS, LANES), f32),
            pltpu.VMEM((3, rows, cols), f32),
            pltpu.VMEM((rows, cols), f32),
            pltpu.SemaphoreType.DMA((3,)),
            pltpu.SemaphoreType.DMA((10,)),
            pltpu.SemaphoreType.DMA((2, 2, PIECES)),
            pltpu.SemaphoreType.DMA((2, 2, PIECES)),
            pltpu.SemaphoreType.DMA((2, 2)),
            pltpu.SemaphoreType.DMA((2, 2)),
            pltpu.SemaphoreType.DMA((2,)),
            pltpu.SemaphoreType.DMA((2,)),
            pltpu.SemaphoreType.DMA((2, chips)),
            pltpu.SemaphoreType.DMA((2, chips)),
            pltpu.SemaphoreType.DMA((2, chips)),
            pltpu.SemaphoreType.DMA((2, chips)),
            pltpu.SemaphoreType.DMA((2,)),
            pltpu.SemaphoreType.DMA((2,)),
        ],
        compiler_params=pltpu.CompilerParams(
            collective_id=0, has_side_effects=True, vmem_limit_bytes=48 * 1024 * 1024
        ),
    )(pressure_now, pressure_old, solid_flags)


def solution(mesh):
    return jax.shard_map(
        shards,
        mesh=mesh,
        in_specs=(P("depth", "tile", None), P("depth", "tile", None), P("depth", "tile", None)),
        out_specs=(P("depth", "tile", None), P("depth", "tile", None), P(None, "tile", None)),
        check_vma=False,
    )
```

time: 55.2 us -> 39.9 us (0.72)
  Pallas kernels: 50.9 us -> 35.2 us
    pallas_call x1, Pallas kernels: 50.9 us -> 35.2 us  [shards(): pl.pallas_call(functools.partial(kernel, 4.0 / (planes * lax.axis_size('d...]
where the time goes in v2:
time: 39.9 us; the launch traced here: 39.5 us
  Pallas kernels  35.2 us (88%)
  local copies, waits for them, and re-layouts  3.61 us (9%)
  between operations  0.64 us (2%)
    pallas_call x1, Pallas kernels, shards(): pl.pallas_call(functools.partial(kernel, 4.0 / (planes * lax.axis_size('d...  35.2 us
    unnamed x3, local copies, waits for them, and re-layouts  3.61 us

profile of v2, /device:TPU:1, one launch (start us, length us, event | category | flops | bytes accessed | tf_op | source)
XLA Modules:
  0.0 39.5 jit_solution(15898797380045687841)
XLA Ops:
  0.6 35.2 %shard_map.58 = (f32[8,64,1024]{2,1,0:T(8,128)S(1)}, f32[8,64,1024]{2,1,0:T(8,128)S(1)}, f32[4,64,1024]{2,1,0:T(8,128)S(1)}) custom-call(f32[8,64,1024]{2,1,0:T(8,128)} %now_h.1, f32[8,64,1024]{2,1,0:T(8,128)} %old_h.1, s32[8,64,1024]{2,1,0:T(8,128)} %flag_h.1), custom_call_target="tpu_custom_call" | custom-call | tf_op jit(solution)/shard_map/pallas_call | solution.py:400
  35.9 1.3 %copy.9 = f32[8,64,1024]{2,1,0:T(8,128)} copy(f32[8,64,1024]{2,1,0:T(8,128)S(1)} %get-tuple-element.6) | data formatting | bytes 4194304
  37.2 1.3 %copy.10 = f32[8,64,1024]{2,1,0:T(8,128)} copy(f32[8,64,1024]{2,1,0:T(8,128)S(1)} %get-tuple-element.7) | data formatting | bytes 4194304
  38.5 1.0 %copy.11 = f32[4,64,1024]{2,1,0:T(8,128)} copy(f32[4,64,1024]{2,1,0:T(8,128)S(1)} %get-tuple-element.8) | data formatting | bytes 2097152

commit v3 on v2

v3 whole, which is shorter than its diff:
```python
import functools
import math

import jax
import jax.numpy as jnp
from jax import lax
from jax.experimental import pallas as pl
from jax.experimental.pallas import tpu as pltpu
from jax.sharding import PartitionSpec as P

MESH = pl.DeviceIdType.MESH
LANES = 128
ROWS = 8
SPREAD = 8
PIECES = 4


def leap(before, field, closed, p, r, l):
    lane = lax.broadcasted_iota(jnp.int32, (ROWS, LANES), 1)
    row = lax.broadcasted_iota(jnp.int32, (ROWS, LANES), 0)

    def tile(dp=0, dr=0, dl=0):
        return field[p + dp, pl.ds(pl.multiple_of(r + dr, ROWS), ROWS), pl.ds(pl.multiple_of(l + dl, LANES), LANES)]

    here = tile()
    west = pltpu.roll(jnp.where(lane == LANES - 1, tile(dl=-LANES), here), 1, 1)
    east = pltpu.roll(jnp.where(lane == 0, tile(dl=LANES), here), LANES - 1, 1)
    north = pltpu.roll(jnp.where(row == ROWS - 1, tile(dr=-ROWS), here), 1, 0)
    south = pltpu.roll(jnp.where(row == 0, tile(dr=ROWS), here), ROWS - 1, 0)
    beside = (tile(dp=-1) + tile(dp=1)) + ((north + south) + (west + east))
    ahead = (0.2 * here - before) + 0.3 * beside
    return jnp.where(closed == 0, ahead, 0.0)


def kernel(
    steps, now_h, old_h, flag_h, mid_out, new, image,
    now, old, flag, mid, part, peer, joint, shares, final,
    load_sem, store_sem, face_send, face_recv, edge_send, edge_recv, pair_send, pair_recv,
    share_send, share_recv, spread_send, spread_recv, swap_send, swap_recv,
):
    depth_count, tile_count = lax.axis_size("depth"), lax.axis_size("tile")
    d, t = lax.axis_index("depth"), lax.axis_index("tile")
    planes, rows, cols = now_h.shape
    blocks, tiles = rows // ROWS, cols // LANES
    chips = depth_count // 2
    core, chip = lax.rem(d, 2), lax.div(d, 2)
    width = math.isqrt(chips)
    piece = rows // PIECES
    d_up, d_down = lax.rem(d + 1, depth_count), lax.rem(d + depth_count - 1, depth_count)
    t_up, t_down = lax.rem(t + 1, tile_count), lax.rem(t + tile_count - 1, tile_count)
    has_d_up, has_d_down = d < depth_count - 1, d > 0
    has_t_up, has_t_down = t < tile_count - 1, t > 0
    partner = d + 1 - 2 * core
    inner_rows, inner_cols = pl.ds(ROWS, rows), pl.ds(LANES, cols)
    near = (
        (has_d_up, (d_up, t)),
        (has_d_down, (d_down, t)),
        (has_t_up, (d, t_up)),
        (has_t_down, (d, t_down)),
    )

    barrier = pltpu.get_barrier_semaphore()
    for there, who in near:

        @pl.when(there)
        def _():
            pl.semaphore_signal(barrier, inc=1, device_id=who, device_id_type=MESH)

    def load(q):
        at = pl.ds(q * piece, piece)
        return [
            pltpu.make_async_copy(src.at[:, at], dst, load_sem.at[q])
            for src, dst in (
                (now_h, now.at[pl.ds(1, planes), pl.ds(ROWS + q * piece, piece), inner_cols]),
                (old_h, old.at[:, at]),
                (flag_h, flag.at[:, at]),
            )
        ]

    def await_load(q):
        three = old.at[:, pl.ds(0, 3 * piece)]
        pltpu.make_async_copy(three, three, load_sem.at[q]).wait()

    for q in range(PIECES):
        for copy in load(q):
            copy.start()

    for k in range(1, chips):
        other = lax.rem(chip + k, chips) * 2 + core
        pl.semaphore_signal(barrier, inc=1, device_id=(other, t), device_id_type=MESH)

    count = chips - 1
    for left in (d, depth_count - 1 - d, t, tile_count - 1 - t):
        count = count + jnp.minimum(left, 1)
    pl.semaphore_wait(barrier, count)

    def depth_face(stage, way, q):
        plane = (planes - 1) * way
        if stage == 0:
            src, field = now_h.at[plane, pl.ds(q * piece, piece)], now
        else:
            src, field = mid.at[plane + 1, pl.ds(ROWS + q * piece, piece), inner_cols], mid
        return pltpu.make_async_remote_copy(
            src_ref=src,
            dst_ref=field.at[(planes + 1) * (1 - way), pl.ds(ROWS + q * piece, piece), inner_cols],
            send_sem=face_send.at[way],
            recv_sem=face_recv.at[stage, way, q],
            device_id=((d_down, d_up)[way], t),
            device_id_type=MESH,
        )

    def tile_face(stage, way):
        row = (rows - 1) * way
        if stage == 0:
            src, field = now_h.at[:, pl.ds(row, 1)], now
        else:
            src, field = mid.at[pl.ds(1, planes), pl.ds(ROWS + row, 1), inner_cols], mid
        return pltpu.make_async_remote_copy(
            src_ref=src,
            dst_ref=field.at[pl.ds(1, planes), pl.ds(ROWS + rows if way == 0 else ROWS - 1, 1), inner_cols],
            send_sem=edge_send.at[way],
            recv_sem=edge_recv.at[stage, way],
            device_id=(d, (t_down, t_up)[way]),
            device_id_type=MESH,
        )

    d_to, t_to = (has_d_down, has_d_up), (has_t_down, has_t_up)
    d_from, t_from = d_to[::-1], t_to[::-1]

    def start_depth(stage, q):
        for way in range(2):
            pl.when(d_to[way])(lambda: depth_face(stage, way, q).start())

    def start_tile(stage, way):
        pl.when(t_to[way])(lambda: tile_face(stage, way).start())

    def await_depth(stage, q):
        for way in range(2):
            pl.when(d_from[way])(lambda: depth_face(stage, way, q).wait_recv())

    def await_tile(stage, way):
        pl.when(t_from[way])(lambda: tile_face(stage, way).wait_recv())

    for way in range(2):
        start_tile(0, way)
    for q in range(PIECES):
        start_depth(0, q)

    for field in (now, mid):
        for side in (0, LANES + cols):
            field[pl.ds(1, planes), inner_rows, pl.ds(side, LANES)] = jnp.zeros((planes, rows, LANES), jnp.float32)

        @pl.when(jnp.logical_not(has_d_down))
        def _():
            field[0, inner_rows, inner_cols] = jnp.zeros((rows, cols), jnp.float32)

        @pl.when(jnp.logical_not(has_d_up))
        def _():
            field[planes + 1, inner_rows, inner_cols] = jnp.zeros((rows, cols), jnp.float32)

        @pl.when(jnp.logical_not(has_t_down))
        def _():
            field[pl.ds(1, planes), pl.ds(0, ROWS), inner_cols] = jnp.zeros((planes, ROWS, cols), jnp.float32)

        @pl.when(jnp.logical_not(has_t_up))
        def _():
            field[pl.ds(1, planes), pl.ds(ROWS + rows, ROWS), inner_cols] = jnp.zeros((planes, ROWS, cols), jnp.float32)

    def over(count, body):
        turns = tiles // SPREAD

        def lap(n, carry):
            i, j = lax.div(n, turns), lax.rem(n, turns)
            for s in range(SPREAD):
                body(i, pl.multiple_of((j * SPREAD + s) * LANES, LANES))
            return carry

        lax.fori_loop(0, count * turns, lap, 0)

    def mid_tile(p, b, l):
        r = pl.multiple_of(b * ROWS, ROWS)
        here = (pl.ds(r, ROWS), pl.ds(l, LANES))
        mid[p + 1, pl.ds(pl.multiple_of(r + ROWS, ROWS), ROWS), pl.ds(pl.multiple_of(l + LANES, LANES), LANES)] = leap(
            old[(p,) + here], now, flag[(p,) + here], p + 1, r + ROWS, l + LANES
        )

    def mid_inner(b, l):
        for p in range(1, planes - 1):
            mid_tile(p, b, l)

    def mid_outer(b, l):
        for p in (0, planes - 1):
            mid_tile(p, b, l)

    rate = steps * math.log2(math.e)

    def new_tile(p, b, l):
        r = pl.multiple_of(b * ROWS, ROWS)
        here = (pl.ds(r, ROWS), pl.ds(l, LANES))
        before = now[p + 1, pl.ds(pl.multiple_of(r + ROWS, ROWS), ROWS), pl.ds(pl.multiple_of(l + LANES, LANES), LANES)]
        value = leap(before, mid, flag[(p,) + here], p + 1, r + ROWS, l + LANES)
        new[(p,) + here] = value
        square = value * value
        thick = square * pltpu.reciprocal(1.0 + square, approx=True)
        return thick, jnp.tanh(1.5 * value), jnp.exp2((-0.5 * math.log2(math.e)) * square)

    def place(b, l):
        return (pl.ds(pl.multiple_of(b * ROWS, ROWS), ROWS), pl.ds(l, LANES))

    def inner(b, l):
        at = place(b, l)
        depth = light = red = green = None
        for p in range(1, planes - 1):
            thick, warm, mild = new_tile(p, b, l)
            if depth is None:
                depth = thick
                after = jnp.exp2(-rate * depth)
                weight = 1.0 - after
                red, green = weight * warm, weight * mild
            else:
                depth = depth + thick
                after = jnp.exp2(-rate * depth)
                weight = light - after
                red, green = red + weight * warm, green + weight * mild
            light = after
        part[(0,) + at], part[(1,) + at], part[(2,) + at] = red, green, depth

    def outer(b, l):
        at = place(b, l)
        depth = part[(2,) + at]
        thick_a, warm_a, mild_a = new_tile(0, b, l)
        thick_b, warm_b, mild_b = new_tile(planes - 1, b, l)
        light_a = jnp.exp2(-rate * thick_a)
        depth_b = thick_a + depth
        light_b = jnp.exp2(-rate * depth_b)
        depth_c = depth_b + thick_b
        light_c = jnp.exp2(-rate * depth_c)
        weight_a, weight_b = 1.0 - light_a, light_b - light_c
        part[(0,) + at] = weight_a * warm_a + light_a * part[(0,) + at] + weight_b * warm_b
        part[(1,) + at] = weight_a * mild_a + light_a * part[(1,) + at] + weight_b * mild_b
        part[(2,) + at] = depth_c

    per = blocks // PIECES
    await_load(0)
    for q in range(1, PIECES):
        await_load(q)
        over(per, lambda i, l: mid_inner((q - 1) * per + 1 + i, l))
    for way in range(2):
        await_tile(0, way)
    over(2, lambda i, l: mid_inner(i * (blocks - 1), l))
    for q in range(PIECES):
        await_depth(0, q)
        over(per, lambda i, l: mid_outer(q * per + i, l))
        start_depth(1, q)
        if q == 0:
            start_tile(1, 0)
        else:
            if q == PIECES - 1:
                start_tile(1, 1)
            over(per, lambda i, l: inner((q - 1) * per + 1 + i, l))
    mid_store = pltpu.make_async_copy(mid.at[pl.ds(1, planes), inner_rows, inner_cols], mid_out, store_sem)
    mid_store.start()

    x, y = lax.div(chip, width), lax.rem(chip, width)
    own_tile = x * 2 + lax.div(y, 2)

    def owner(s, j):
        ox = lax.div(j, 2)
        return ox * width + 2 * lax.rem(j, 2) + lax.rem(ox + s, 2)

    def owns(s):
        return lax.rem(x + y + s, 2) == 0

    def block_rows(s, whose):
        return pl.ds(pl.multiple_of((2 * s + whose) * ROWS, ROWS), ROWS)

    def tile_cols(j):
        return pl.ds(pl.multiple_of(j * LANES, LANES), LANES)

    def pair(s):
        return pltpu.make_async_remote_copy(
            src_ref=part.at[:, block_rows(s, 1 - core)],
            dst_ref=peer.at[s],
            send_sem=pair_send,
            recv_sem=pair_recv.at[s],
            device_id=(partner, t),
            device_id_type=MESH,
        )

    def share(s, j):
        return pltpu.make_async_remote_copy(
            src_ref=joint.at[s, :, :, tile_cols(j)],
            dst_ref=shares.at[s, chip],
            send_sem=share_send,
            recv_sem=share_recv.at[s],
            device_id=(owner(s, j) * 2 + core, t),
            device_id_type=MESH,
        )

    def region(s, j):
        return final.at[:, block_rows(s, core), tile_cols(j)]

    def spread(s, who):
        return pltpu.make_async_remote_copy(
            src_ref=region(s, own_tile),
            dst_ref=region(s, own_tile),
            send_sem=spread_send,
            recv_sem=spread_recv.at[s],
            device_id=(who * 2 + core, t),
            device_id_type=MESH,
        )

    def swap(s, whose):
        at = final.at[:, block_rows(s, whose)]
        return pltpu.make_async_remote_copy(
            src_ref=at,
            dst_ref=at,
            send_sem=swap_send,
            recv_sem=swap_recv.at[s],
            device_id=(partner, t),
            device_id_type=MESH,
        )

    def await_tiles(sem, count):
        some = shares.at[pl.ds(0, 2), pl.ds(0, count // 2)] if count > chips else shares.at[0, pl.ds(0, count)]
        pltpu.make_async_copy(some, some, sem).wait()

    def shade(s):
        if s == 0:
            await_tile(1, 1)
            over(1, lambda _, l: inner(0, l))
        if s == PIECES - 1:
            await_tile(1, 0)
            over(1, lambda _, l: inner(blocks - 1, l))
        await_depth(1, s)
        over(1, lambda _, l: outer(2 * s + 1 - core, l))
        pair(s).start()
        over(1, lambda _, l: outer(2 * s + core, l))

    def join(s):
        pair(s).wait_recv()

        def merge(_, l):
            mine, first = (block_rows(s, core), pl.ds(l, LANES)), core == 0
            theirs = (slice(None), pl.ds(l, LANES))
            own = [part[(c,) + mine] for c in range(3)]
            other = [peer[(s, c) + theirs] for c in range(3)]
            light = jnp.exp2(-rate * jnp.where(first, own[2], other[2]))
            for c in range(2):
                joint[(s, c) + theirs] = jnp.where(first, own[c], other[c]) + light * jnp.where(first, other[c], own[c])
            joint[(s, 2) + theirs] = own[2] + other[2]

        over(1, merge)
        for k in range(tiles):
            j = lax.rem(chip + k, tiles)
            pl.when(owner(s, j) != chip)(lambda: share(s, j).start())

        @pl.when(owns(s))
        def _():
            for c in range(3):
                shares[s, chip, c] = joint[s, c, :, tile_cols(own_tile)]

    def compose(s):
        @pl.when(owns(s))
        def _():
            await_tiles(share_recv.at[s], chips - 1)
            red, green, depth = (shares[s, 0, c] for c in range(3))
            for k in range(1, chips):
                light = jnp.exp2(-rate * depth)
                red, green = red + light * shares[s, k, 0], green + light * shares[s, k, 1]
                depth = depth + shares[s, k, 2]
            opacity = 1.0 - jnp.exp2(-rate * depth)
            for c, value in enumerate((0.5 * (opacity + red), green, opacity)):
                final[c, block_rows(s, core), tile_cols(own_tile)] = value
            for k in range(1, chips):
                spread(s, lax.rem(chip + k, chips)).start()

    def gather(s):
        pl.when(owns(s))(lambda: await_tiles(spread_recv.at[s], tiles - 1))
        pl.when(jnp.logical_not(owns(s)))(lambda: await_tiles(spread_recv.at[s], tiles))
        swap(s, core).start()

    def finish(s):
        swap(s, 1 - core).wait_recv()
        at = pl.ds(2 * s * ROWS, 2 * ROWS)
        red, green, opacity = (final[c, at] for c in range(3))
        for c, value in enumerate((red, green, opacity - red, opacity)):
            image[c, at] = value

    shade(0)
    for s in range(1, PIECES):
        shade(s)
        join(s - 1)
    join(PIECES - 1)
    for s in range(PIECES):
        compose(s)
    for s in range(PIECES):
        gather(s)
        if s > 0:
            finish(s - 1)
    finish(PIECES - 1)

    def sent(like, sem):
        pltpu.make_async_copy(like, like, sem).wait()

    for way in range(2):
        pl.when(d_to[way])(lambda: sent(now.at[pl.ds(0, 2), inner_rows, inner_cols], face_send.at[way]))
        pl.when(t_to[way])(lambda: sent(old.at[0, pl.ds(0, 2 * planes)], edge_send.at[way]))
    sent(peer, pair_send)
    await_tiles(share_send, PIECES * tiles - 2)
    await_tiles(spread_send, 2 * (chips - 1))
    sent(peer, swap_send)
    mid_store.wait()


def shards(pressure_old, pressure_now, solid_flags):
    planes, rows, cols = pressure_now.shape
    chips = lax.axis_size("depth") // 2
    any_space = pl.BlockSpec(memory_space=pl.ANY)
    f32 = jnp.float32
    halo = (planes + 2, rows + 2 * ROWS, cols + 2 * LANES)
    return pl.pallas_call(
        functools.partial(kernel, 4.0 / (planes * lax.axis_size("depth"))),
        out_shape=[
            jax.ShapeDtypeStruct(pressure_now.shape, f32),
            jax.ShapeDtypeStruct(pressure_now.shape, f32),
            jax.ShapeDtypeStruct((4, rows, cols), f32),
        ],
        in_specs=[any_space] * 3,
        out_specs=[pl.BlockSpec(memory_space=pltpu.VMEM)] * 3,
        scratch_shapes=[
            pltpu.VMEM(halo, f32),
            pltpu.VMEM(pressure_now.shape, f32),
            pltpu.VMEM(pressure_now.shape, jnp.int32),
            pltpu.VMEM(halo, f32),
            pltpu.VMEM((3, rows, cols), f32),
            pltpu.VMEM((PIECES, 3, ROWS, cols), f32),
            pltpu.VMEM((PIECES, 3, ROWS, cols), f32),
            pltpu.VMEM((PIECES, chips, 3, ROWS, LANES), f32),
            pltpu.VMEM((3, rows, cols), f32),
            pltpu.SemaphoreType.DMA((PIECES,)),
            pltpu.SemaphoreType.DMA,
            pltpu.SemaphoreType.DMA((2,)),
            pltpu.SemaphoreType.DMA((2, 2, PIECES)),
            pltpu.SemaphoreType.DMA((2,)),
            pltpu.SemaphoreType.DMA((2, 2)),
            pltpu.SemaphoreType.DMA,
            pltpu.SemaphoreType.DMA((PIECES,)),
            pltpu.SemaphoreType.DMA,
            pltpu.SemaphoreType.DMA((PIECES,)),
            pltpu.SemaphoreType.DMA,
            pltpu.SemaphoreType.DMA((PIECES,)),
            pltpu.SemaphoreType.DMA,
            pltpu.SemaphoreType.DMA((PIECES,)),
        ],
        compiler_params=pltpu.CompilerParams(
            collective_id=0, has_side_effects=True, vmem_limit_bytes=48 * 1024 * 1024
        ),
    )(pressure_now, pressure_old, solid_flags)


def solution(mesh):
    return jax.shard_map(
        shards,
        mesh=mesh,
        in_specs=(P("depth", "tile", None), P("depth", "tile", None), P("depth", "tile", None)),
        out_specs=(P("depth", "tile", None), P("depth", "tile", None), P(None, "tile", None)),
        check_vma=False,
    )
```

time: 39.9 us -> 36.9 us (0.925)
  the two profiles are of different devices: /device:TPU:1 before, /device:TPU:129 now
where the time goes in v3:
time: 36.9 us; the launch traced here: 36.8 us
  Pallas kernels  32.6 us (88%)
  local copies, waits for them, and re-layouts  3.61 us (10%)
  between operations  0.64 us (2%)
    pallas_call x1, Pallas kernels, shards(): pl.pallas_call(functools.partial(kernel, 4.0 / (planes * lax.axis_size('d...  32.6 us
    unnamed x3, local copies, waits for them, and re-layouts  3.61 us

profile of v3, /device:TPU:129, one launch (start us, length us, event | category | flops | bytes accessed | tf_op | source)
XLA Modules:
  0.0 36.8 jit_solution(4664203491204903365)
XLA Ops:
  0.6 32.6 %shard_map.58 = (f32[8,64,1024]{2,1,0:T(8,128)S(1)}, f32[8,64,1024]{2,1,0:T(8,128)S(1)}, f32[4,64,1024]{2,1,0:T(8,128)S(1)}) custom-call(f32[8,64,1024]{2,1,0:T(8,128)} %now_h.1, f32[8,64,1024]{2,1,0:T(8,128)} %old_h.1, s32[8,64,1024]{2,1,0:T(8,128)} %flag_h.1), custom_call_target="tpu_custom_call" | custom-call | tf_op jit(solution)/shard_map/pallas_call | solution.py:422
  33.2 1.3 %copy.9 = f32[8,64,1024]{2,1,0:T(8,128)} copy(f32[8,64,1024]{2,1,0:T(8,128)S(1)} %get-tuple-element.6) | data formatting | bytes 4194304
  34.5 1.3 %copy.10 = f32[8,64,1024]{2,1,0:T(8,128)} copy(f32[8,64,1024]{2,1,0:T(8,128)S(1)} %get-tuple-element.7) | data formatting | bytes 4194304
  35.9 1.0 %copy.11 = f32[4,64,1024]{2,1,0:T(8,128)} copy(f32[4,64,1024]{2,1,0:T(8,128)S(1)} %get-tuple-element.8) | data formatting | bytes 2097152

commit v4 on v3

--- a/solution.py
+++ b/solution.py
@@ -33,9 +33,9 @@
 
 
 def kernel(
-    steps, now_h, old_h, flag_h, mid_out, new, image,
-    now, old, flag, mid, part, peer, joint, shares, final,
-    load_sem, store_sem, face_send, face_recv, edge_send, edge_recv, pair_send, pair_recv,
+    steps, now_h, old_h, flag_h, mid, new, final,
+    now, old, flag, part, peer, joint, shares,
+    load_sem, face_send, face_recv, edge_send, edge_recv, pair_send, pair_recv,
     share_send, share_recv, spread_send, spread_recv, swap_send, swap_recv,
 ):
     depth_count, tile_count = lax.axis_size("depth"), lax.axis_size("tile")
@@ -258,8 +258,6 @@
             if q == PIECES - 1:
                 start_tile(1, 1)
             over(per, lambda i, l: inner((q - 1) * per + 1 + i, l))
-    mid_store = pltpu.make_async_copy(mid.at[pl.ds(1, planes), inner_rows, inner_cols], mid_out, store_sem)
-    mid_store.start()
 
     x, y = lax.div(chip, width), lax.rem(chip, width)
     own_tile = x * 2 + lax.div(y, 2)
@@ -380,13 +378,6 @@
         pl.when(jnp.logical_not(owns(s)))(lambda: await_tiles(spread_recv.at[s], tiles))
         swap(s, core).start()
 
-    def finish(s):
-        swap(s, 1 - core).wait_recv()
-        at = pl.ds(2 * s * ROWS, 2 * ROWS)
-        red, green, opacity = (final[c, at] for c in range(3))
-        for c, value in enumerate((red, green, opacity - red, opacity)):
-            image[c, at] = value
-
     shade(0)
     for s in range(1, PIECES):
         shade(s)
@@ -396,9 +387,8 @@
         compose(s)
     for s in range(PIECES):
         gather(s)
-        if s > 0:
-            finish(s - 1)
-    finish(PIECES - 1)
+    for s in range(PIECES):
+        swap(s, 1 - core).wait_recv()
 
     def sent(like, sem):
         pltpu.make_async_copy(like, like, sem).wait()
@@ -410,36 +400,52 @@
     await_tiles(share_send, PIECES * tiles - 2)
     await_tiles(spread_send, 2 * (chips - 1))
     sent(peer, swap_send)
-    mid_store.wait()
+
+
+def store(mid, new, final, mid_h, new_h, image_h, blue, sems):
+    planes, rows, cols = new.shape
+    pairs = (
+        (final.at[0], image_h.at[0]),
+        (final.at[1], image_h.at[1]),
+        (final.at[2], image_h.at[3]),
+        (mid.at[pl.ds(1, planes), pl.ds(ROWS, rows), pl.ds(LANES, cols)], mid_h),
+        (new, new_h),
+        (blue, image_h.at[2]),
+    )
+    copies = [pltpu.make_async_copy(src, dst, sems.at[i]) for i, (src, dst) in enumerate(pairs)]
+    for copy in copies[:-1]:
+        copy.start()
+    blue[...] = final[2] - final[0]
+    copies[-1].start()
+    for copy in copies:
+        copy.wait()
 
 
 def shards(pressure_old, pressure_now, solid_flags):
     planes, rows, cols = pressure_now.shape
     chips = lax.axis_size("depth") // 2
     any_space = pl.BlockSpec(memory_space=pl.ANY)
+    vmem_space = pl.BlockSpec(memory_space=pltpu.VMEM)
     f32 = jnp.float32
     halo = (planes + 2, rows + 2 * ROWS, cols + 2 * LANES)
-    return pl.pallas_call(
+    mid, new, final = pl.pallas_call(
         functools.partial(kernel, 4.0 / (planes * lax.axis_size("depth"))),
         out_shape=[
+            jax.ShapeDtypeStruct(halo, f32),
             jax.ShapeDtypeStruct(pressure_now.shape, f32),
-            jax.ShapeDtypeStruct(pressure_now.shape, f32),
-            jax.ShapeDtypeStruct((4, rows, cols), f32),
+            jax.ShapeDtypeStruct((3, rows, cols), f32),
         ],
         in_specs=[any_space] * 3,
-        out_specs=[pl.BlockSpec(memory_space=pltpu.VMEM)] * 3,
+        out_specs=[vmem_space] * 3,
         scratch_shapes=[
             pltpu.VMEM(halo, f32),
             pltpu.VMEM(pressure_now.shape, f32),
             pltpu.VMEM(pressure_now.shape, jnp.int32),
-            pltpu.VMEM(halo, f32),
             pltpu.VMEM((3, rows, cols), f32),
             pltpu.VMEM((PIECES, 3, ROWS, cols), f32),
             pltpu.VMEM((PIECES, 3, ROWS, cols), f32),
             pltpu.VMEM((PIECES, chips, 3, ROWS, LANES), f32),
-            pltpu.VMEM((3, rows, cols), f32),
             pltpu.SemaphoreType.DMA((PIECES,)),
-            pltpu.SemaphoreType.DMA,
             pltpu.SemaphoreType.DMA((2,)),
             pltpu.SemaphoreType.DMA((2, 2, PIECES)),
             pltpu.SemaphoreType.DMA((2,)),
@@ -457,6 +463,17 @@
             collective_id=0, has_side_effects=True, vmem_limit_bytes=48 * 1024 * 1024
         ),
     )(pressure_now, pressure_old, solid_flags)
+    return pl.pallas_call(
+        store,
+        out_shape=[
+            jax.ShapeDtypeStruct(pressure_now.shape, f32),
+            jax.ShapeDtypeStruct(pressure_now.shape, f32),
+            jax.ShapeDtypeStruct((4, rows, cols), f32),
+        ],
+        in_specs=[vmem_space] * 3,
+        out_specs=[any_space] * 3,
+        scratch_shapes=[pltpu.VMEM((rows, cols), f32), pltpu.SemaphoreType.DMA((6,))],
+    )(mid, new, final)
 
 
 def solution(mesh):

time: 36.9 us -> 44.1 us (1.20)
  Pallas kernels: 32.6 us -> 39.5 us
    pallas_call x0 -> x1, Pallas kernels: none -> 5.34 us  [shards(): pl.pallas_call(store, out_shape=[jax.ShapeDtypeStruct(pressure_now.shape,...]
    pallas_call x1, Pallas kernels: 32.6 us -> 34.2 us  [shards(): pl.pallas_call(functools.partial(kernel, 4.0 / (planes * lax.axis_size('d...]
    unnamed x3 -> x6, local copies, waits for them, and re-layouts: 3.61 us -> 3.79 us
where the time goes in v4:
time: 44.1 us; the launch traced here: 44 us
  Pallas kernels  39.5 us (90%)
  local copies, waits for them, and re-layouts  3.79 us (9%)
  between operations  0.66 us (1%)
    pallas_call x1, Pallas kernels, shards(): pl.pallas_call(functools.partial(kernel, 4.0 / (planes * lax.axis_size('d...  34.2 us
    pallas_call x1, Pallas kernels, shards(): pl.pallas_call(store, out_shape=[jax.ShapeDtypeStruct(pressure_now.shape,...  5.34 us
    unnamed x6, local copies, waits for them, and re-layouts  3.79 us

profile of v4, /device:TPU:129, one launch (start us, length us, event | category | flops | bytes accessed | tf_op | source)
XLA Modules:
  0.0 44.0 jit_solution(16194597914067393049)
XLA Ops:
  0.6 0.0 copy-start
  0.6 1.6 %copy-done = f32[8,64,1024]{2,1,0:T(8,128)S(1)} copy-done((f32[8,64,1024]{2,1,0:T(8,128)S(1)}, f32[8,64,1024]{2,1,0:T(8,128)}, u32[]{:S(2)}) %copy-start) | copy-done | bytes 2097176
  2.2 34.2 %shard_map.58 = (f32[10,80,1280]{2,1,0:T(8,128)}, f32[8,64,1024]{2,1,0:T(8,128)S(1)}, f32[3,64,1024]{2,1,0:T(8,128)S(1)}) custom-call(f32[8,64,1024]{2,1,0:T(8,128)S(1)} %copy-done, f32[8,64,1024]{2,1,0:T(8,128)} %old_h.1, s32[8,64,1024]{2,1,0:T(8,128)} %flag_h.1), custom_call_target="tpu_custom_call" | custom-call | tf_op jit(solution)/shard_map/pallas_call | solution.py:431
  36.4 0.0 copy-start.1
  36.4 1.3 %copy-done.1 = f32[8,64,1024]{2,1,0:T(8,128)} copy-done((f32[8,64,1024]{2,1,0:T(8,128)}, f32[8,64,1024]{2,1,0:T(8,128)S(1)}, u32[]{:S(2)}) %copy-start.1) | copy-done | bytes 2097176
  37.7 0.0 copy-start.2
  37.7 0.9 %copy-done.2 = f32[3,64,1024]{2,1,0:T(8,128)} copy-done((f32[3,64,1024]{2,1,0:T(8,128)}, f32[3,64,1024]{2,1,0:T(8,128)S(1)}, u32[]{:S(2)}) %copy-start.2) | copy-done | bytes 786456
  38.6 5.3 %shard_map.59 = (f32[8,64,1024]{2,1,0:T(8,128)}, f32[8,64,1024]{2,1,0:T(8,128)}, f32[4,64,1024]{2,1,0:T(8,128)}) custom-call(f32[10,80,1280]{2,1,0:T(8,128)} %get-tuple-element.6.mid, f32[8,64,1024]{2,1,0:T(8,128)} %copy-done.1, f32[3,64,1024]{2,1,0:T(8,128)} %copy-done.2), custom_call_target="tpu_custom_call" | custom-call | tf_op jit(solution)/shard_map/pallas_call | solution.py:466
Async XLA Ops:
  0.6 1.6 %copy-start = (f32[8,64,1024]{2,1,0:T(8,128)S(1)}, f32[8,64,1024]{2,1,0:T(8,128)}, u32[]{:S(2)}) copy-start(f32[8,64,1024]{2,1,0:T(8,128)} %now_h.1) | copy-start | bytes 6291460
  36.4 1.3 %copy-start.1 = (f32[8,64,1024]{2,1,0:T(8,128)}, f32[8,64,1024]{2,1,0:T(8,128)S(1)}, u32[]{:S(2)}) copy-start(f32[8,64,1024]{2,1,0:T(8,128)S(1)} %get-tuple-element.7.new) | copy-start | bytes 6291460
  37.7 0.9 %copy-start.2 = (f32[3,64,1024]{2,1,0:T(8,128)}, f32[3,64,1024]{2,1,0:T(8,128)S(1)}, u32[]{:S(2)}) copy-start(f32[3,64,1024]{2,1,0:T(8,128)S(1)} %get-tuple-element.8.final) | copy-start | bytes 2359300

commit v5 on v3

--- a/solution.py
+++ b/solution.py
@@ -12,10 +12,11 @@
 LANES = 128
 ROWS = 8
 SPREAD = 8
+FAR_FIRST = (2, 1, 3, 0)
 PIECES = 4
 
 
-def leap(before, field, closed, p, r, l):
+def leap(before, field, closed, p, r, l, above=True, below=True):
     lane = lax.broadcasted_iota(jnp.int32, (ROWS, LANES), 1)
     row = lax.broadcasted_iota(jnp.int32, (ROWS, LANES), 0)
 
@@ -25,8 +26,8 @@
     here = tile()
     west = pltpu.roll(jnp.where(lane == LANES - 1, tile(dl=-LANES), here), 1, 1)
     east = pltpu.roll(jnp.where(lane == 0, tile(dl=LANES), here), LANES - 1, 1)
-    north = pltpu.roll(jnp.where(row == ROWS - 1, tile(dr=-ROWS), here), 1, 0)
-    south = pltpu.roll(jnp.where(row == 0, tile(dr=ROWS), here), ROWS - 1, 0)
+    north = pltpu.roll(jnp.where(row == ROWS - 1, tile(dr=-ROWS), here) if above else here, 1, 0)
+    south = pltpu.roll(jnp.where(row == 0, tile(dr=ROWS), here) if below else here, ROWS - 1, 0)
     beside = (tile(dp=-1) + tile(dp=1)) + ((north + south) + (west + east))
     ahead = (0.2 * here - before) + 0.3 * beside
     return jnp.where(closed == 0, ahead, 0.0)
@@ -177,20 +178,19 @@
 
         lax.fori_loop(0, count * turns, lap, 0)
 
-    def mid_tile(p, b, l):
+    def mid_tile(p, b, l, above=True, below=True):
         r = pl.multiple_of(b * ROWS, ROWS)
         here = (pl.ds(r, ROWS), pl.ds(l, LANES))
         mid[p + 1, pl.ds(pl.multiple_of(r + ROWS, ROWS), ROWS), pl.ds(pl.multiple_of(l + LANES, LANES), LANES)] = leap(
-            old[(p,) + here], now, flag[(p,) + here], p + 1, r + ROWS, l + LANES
-        )
-
-    def mid_inner(b, l):
-        for p in range(1, planes - 1):
-            mid_tile(p, b, l)
-
-    def mid_outer(b, l):
-        for p in (0, planes - 1):
-            mid_tile(p, b, l)
+            old[(p,) + here], now, flag[(p,) + here], p + 1, r + ROWS, l + LANES, above, below
+        )
+
+    def mid_blocks(first, count, chosen, above=True, below=True):
+        def body(i, l):
+            for p in chosen:
+                mid_tile(p, first + i, l, above, below)
+
+        over(count, body)
 
     rate = steps * math.log2(math.e)
 
@@ -240,24 +240,35 @@
         part[(1,) + at] = weight_a * mild_a + light_a * part[(1,) + at] + weight_b * mild_b
         part[(2,) + at] = depth_c
 
-    per = blocks // PIECES
+    within, ends = range(1, planes - 1), (0, planes - 1)
+    last = blocks - 1
     await_load(0)
+    mid_blocks(0, 1, within, above=False)
     for q in range(1, PIECES):
         await_load(q)
-        over(per, lambda i, l: mid_inner((q - 1) * per + 1 + i, l))
-    for way in range(2):
-        await_tile(0, way)
-    over(2, lambda i, l: mid_inner(i * (blocks - 1), l))
+        mid_blocks(2 * q - 1, 2, within)
+    mid_blocks(last, 1, within, below=False)
     for q in range(PIECES):
         await_depth(0, q)
-        over(per, lambda i, l: mid_outer(q * per + i, l))
-        start_depth(1, q)
         if q == 0:
+            mid_blocks(0, 1, ends, above=False)
+            mid_blocks(1, 1, ends)
+            continue
+        if q < PIECES - 1:
+            mid_blocks(2 * q, 2, ends)
+            start_depth(1, q)
+        else:
+            mid_blocks(2 * q, 1, ends)
+            await_tile(0, 0)
+            mid_blocks(last, 1, range(planes))
+            start_depth(1, q)
+            start_tile(1, 1)
+        over(2, lambda i, l: inner(2 * q - 1 + i, l))
+        if q == PIECES - 2:
+            await_tile(0, 1)
+            mid_blocks(0, 1, range(planes))
+            start_depth(1, 0)
             start_tile(1, 0)
-        else:
-            if q == PIECES - 1:
-                start_tile(1, 1)
-            over(per, lambda i, l: inner((q - 1) * per + 1 + i, l))
     mid_store = pltpu.make_async_copy(mid.at[pl.ds(1, planes), inner_rows, inner_cols], mid_out, store_sem)
     mid_store.start()
 
@@ -351,9 +362,10 @@
             joint[(s, 2) + theirs] = own[2] + other[2]
 
         over(1, merge)
-        for k in range(tiles):
-            j = lax.rem(chip + k, tiles)
-            pl.when(owner(s, j) != chip)(lambda: share(s, j).start())
+        for dx in FAR_FIRST:
+            for m in range(2):
+                j = 2 * lax.rem(x + dx, width) + lax.rem(lax.div(y, 2) + 1 + m, 2)
+                pl.when(owner(s, j) != chip)(lambda: share(s, j).start())
 
         @pl.when(owns(s))
         def _():
@@ -372,8 +384,10 @@
             opacity = 1.0 - jnp.exp2(-rate * depth)
             for c, value in enumerate((0.5 * (opacity + red), green, opacity)):
                 final[c, block_rows(s, core), tile_cols(own_tile)] = value
-            for k in range(1, chips):
-                spread(s, lax.rem(chip + k, chips)).start()
+            for dx in FAR_FIRST:
+                for dy in FAR_FIRST:
+                    if dx or dy:
+                        spread(s, lax.rem(x + dx, width) * width + lax.rem(y + dy, width)).start()
 
     def gather(s):
         pl.when(owns(s))(lambda: await_tiles(spread_recv.at[s], tiles - 1))
@@ -387,18 +401,19 @@
         for c, value in enumerate((red, green, opacity - red, opacity)):
             image[c, at] = value
 
-    shade(0)
-    for s in range(1, PIECES):
+    order = (1, 2, 0, 3)
+    shade(order[0])
+    for earlier, s in zip(order, order[1:]):
         shade(s)
-        join(s - 1)
-    join(PIECES - 1)
-    for s in range(PIECES):
+        join(earlier)
+    join(order[-1])
+    for s in order:
         compose(s)
-    for s in range(PIECES):
+    gather(order[0])
+    for earlier, s in zip(order, order[1:]):
         gather(s)
-        if s > 0:
-            finish(s - 1)
-    finish(PIECES - 1)
+        finish(earlier)
+    finish(order[-1])
 
     def sent(like, sem):
         pltpu.make_async_copy(like, like, sem).wait()

time: 36.9 us -> 35.9 us (0.973)
  the two profiles are of different devices: /device:TPU:129 before, /device:TPU:1 now
where the time goes in v5:
time: 35.9 us; the launch traced here: 35.8 us
  Pallas kernels  31.6 us (88%)
  local copies, waits for them, and re-layouts  3.61 us (10%)
  between operations  0.64 us (2%)
    pallas_call x1, Pallas kernels, shards(): pl.pallas_call(functools.partial(kernel, 4.0 / (planes * lax.axis_size('d...  31.6 us
    unnamed x3, local copies, waits for them, and re-layouts  3.61 us

profile of v5, /device:TPU:1, one launch (start us, length us, event | category | flops | bytes accessed | tf_op | source)
XLA Modules:
  0.0 35.8 jit_solution(10638513005941590634)
XLA Ops:
  0.6 31.6 %shard_map.58 = (f32[8,64,1024]{2,1,0:T(8,128)S(1)}, f32[8,64,1024]{2,1,0:T(8,128)S(1)}, f32[4,64,1024]{2,1,0:T(8,128)S(1)}) custom-call(f32[8,64,1024]{2,1,0:T(8,128)} %now_h.1, f32[8,64,1024]{2,1,0:T(8,128)} %old_h.1, s32[8,64,1024]{2,1,0:T(8,128)} %flag_h.1), custom_call_target="tpu_custom_call" | custom-call | tf_op jit(solution)/shard_map/pallas_call | solution.py:437
  32.2 1.3 %copy.9 = f32[8,64,1024]{2,1,0:T(8,128)} copy(f32[8,64,1024]{2,1,0:T(8,128)S(1)} %get-tuple-element.6) | data formatting | bytes 4194304
  33.5 1.3 %copy.10 = f32[8,64,1024]{2,1,0:T(8,128)} copy(f32[8,64,1024]{2,1,0:T(8,128)S(1)} %get-tuple-element.7) | data formatting | bytes 4194304
  34.8 1.0 %copy.11 = f32[4,64,1024]{2,1,0:T(8,128)} copy(f32[4,64,1024]{2,1,0:T(8,128)S(1)} %get-tuple-element.8) | data formatting | bytes 2097152

commit v6 on v5

--- a/solution.py
+++ b/solution.py
@@ -61,6 +61,12 @@
     )
 
     barrier = pltpu.get_barrier_semaphore()
+    x, y = lax.div(chip, width), lax.rem(chip, width)
+    for dx in FAR_FIRST:
+        for dy in FAR_FIRST:
+            if dx or dy:
+                other = lax.rem(x + dx, width) * width + lax.rem(y + dy, width)
+                pl.semaphore_signal(barrier, inc=1, device_id=(other * 2 + core, t), device_id_type=MESH)
     for there, who in near:
 
         @pl.when(there)
@@ -85,10 +91,6 @@
     for q in range(PIECES):
         for copy in load(q):
             copy.start()
-
-    for k in range(1, chips):
-        other = lax.rem(chip + k, chips) * 2 + core
-        pl.semaphore_signal(barrier, inc=1, device_id=(other, t), device_id_type=MESH)
 
     count = chips - 1
     for left in (d, depth_count - 1 - d, t, tile_count - 1 - t):
@@ -272,7 +274,6 @@
     mid_store = pltpu.make_async_copy(mid.at[pl.ds(1, planes), inner_rows, inner_cols], mid_out, store_sem)
     mid_store.start()
 
-    x, y = lax.div(chip, width), lax.rem(chip, width)
     own_tile = x * 2 + lax.div(y, 2)
 
     def owner(s, j):

time: 35.9 us -> 35.8 us (level)
  no operation moved by 1% of the time
where the time goes in v6:
time: 35.8 us; the launch traced here: 35.7 us
  Pallas kernels  31.5 us (88%)
  local copies, waits for them, and re-layouts  3.61 us (10%)
  between operations  0.64 us (2%)
    pallas_call x1, Pallas kernels, shards(): pl.pallas_call(functools.partial(kernel, 4.0 / (planes * lax.axis_size('d...  31.5 us
    unnamed x3, local copies, waits for them, and re-layouts  3.61 us

profile of v6, /device:TPU:1, one launch (start us, length us, event | category | flops | bytes accessed | tf_op | source)
XLA Modules:
  0.0 35.7 jit_solution(15886087302085389657)
XLA Ops:
  0.6 31.5 %shard_map.58 = (f32[8,64,1024]{2,1,0:T(8,128)S(1)}, f32[8,64,1024]{2,1,0:T(8,128)S(1)}, f32[4,64,1024]{2,1,0:T(8,128)S(1)}) custom-call(f32[8,64,1024]{2,1,0:T(8,128)} %now_h.1, f32[8,64,1024]{2,1,0:T(8,128)} %old_h.1, s32[8,64,1024]{2,1,0:T(8,128)} %flag_h.1), custom_call_target="tpu_custom_call" | custom-call | tf_op jit(solution)/shard_map/pallas_call | solution.py:438
  32.1 1.3 %copy.9 = f32[8,64,1024]{2,1,0:T(8,128)} copy(f32[8,64,1024]{2,1,0:T(8,128)S(1)} %get-tuple-element.6) | data formatting | bytes 4194304
  33.4 1.3 %copy.10 = f32[8,64,1024]{2,1,0:T(8,128)} copy(f32[8,64,1024]{2,1,0:T(8,128)S(1)} %get-tuple-element.7) | data formatting | bytes 4194304
  34.7 1.0 %copy.11 = f32[4,64,1024]{2,1,0:T(8,128)} copy(f32[4,64,1024]{2,1,0:T(8,128)S(1)} %get-tuple-element.8) | data formatting | bytes 2097152
